TPU v7x, 256 devices: a whole 4x4x8 slice. The times are simulated.
256 devices in a mesh: mode: 8 (over z_hi, x), grid: 32 (over y, z_lo, core).
Axes of the slice: x: 4, y: 4, z: 8 (z_hi: 2, z_lo: 4; z = z_hi * 4 + z_lo), core: 2. Of those that a mesh axis runs over, the one named last changes fastest.
Arguments:
- omega_re: float32 [56, 512, 1024], P('mode', 'grid'), may hold values from -6 to 6
- omega_im: float32 [56, 512, 1024], P('mode', 'grid'), may hold values from -6 to 6
- base_re: float32 [56, 512, 1024], P('mode', 'grid'), may hold values from -6 to 6
- base_im: float32 [56, 512, 1024], P('mode', 'grid'), may hold values from -6 to 6
- triple: bfloat16 [56, 56, 56], replicated, may hold values from -0.109375 to 0.109375
Outputs:
- new_re: float32 [56, 512, 1024], P('mode', 'grid')
- new_im: float32 [56, 512, 1024], P('mode', 'grid')
All inputs are finite; a program needn't handle non-finite values.
Results may differ from a plain program's by a relative error of at most 0.005.
Values may be sent and summed in bfloat16 or wider, within the bound.
No kernel may reach another device: no remote copies, remote signals or barrier semaphores. Data moves between devices by JAX's collectives and lax.ppermute only.
A program may use at most 128 MiB of HBM per device.

v0:
```python
import functools
import math

import jax
import jax.numpy as jnp
import ml_dtypes
import numpy as np
from jax import lax
from jax.experimental import pallas as pl
from jax.experimental.pallas import tpu as pltpu
from jax.sharding import PartitionSpec as P

VISCOSITY = 4.0
STEP_WEIGHT = 0.5
NG = 1024
KEPT = 512
MODES = 56
GROUPS = 8
SLABS = 32
DEVS = GROUPS * SLABS
OWN = MODES // GROUPS
ROWS = KEPT // SLABS
PARTS = NG // DEVS
QUART = NG // 4
FACTOR = 1.0 / math.sqrt(NG)
LIVE = 24
BF = jnp.bfloat16
F32 = jnp.float32
VMEM_LIMIT = 56 * 1024 * 1024


def circle(phases):
    angles = (phases % NG).astype(np.float32) * np.float32(2.0 * math.pi / NG)
    return np.cos(angles), np.sin(angles)


def x_tables():
    ahead, back = [], []
    short = np.arange(QUART)
    for part in range(PARTS):
        points = PARTS * short + part
        cos, sin = circle(short[:, None] * points[None, :])
        ahead.append(np.block([[cos, sin], [-sin, cos]]))
        cos, sin = circle(points[:, None] * short[None, :])
        back.append(np.block([[cos, -sin], [sin, cos]]))
    return (
        np.stack(ahead).astype(ml_dtypes.bfloat16),
        np.stack(back).astype(ml_dtypes.bfloat16),
    )


def y_tables():
    waves = np.arange(KEPT)
    points = np.arange(NG)
    cos, sin = circle(waves[:, None] * points[None, :])
    weights = np.where(waves == 0, 1.0, 2.0).astype(np.float32)[:, None]
    ahead = np.stack([(weights * cos).reshape(SLABS, ROWS, NG), (-weights * sin).reshape(SLABS, ROWS, NG)], axis=1)
    ahead = ahead.reshape(2 * KEPT, NG).astype(ml_dtypes.bfloat16)
    back = np.stack([cos.T.reshape(NG, SLABS, ROWS), -sin.T.reshape(NG, SLABS, ROWS)], axis=2)
    back = back[:, :LIVE].reshape(NG, LIVE * 2 * ROWS).astype(ml_dtypes.bfloat16)
    return ahead, back


def regroup(parts):
    lane = lax.broadcasted_iota(jnp.int32, parts[0].shape, parts[0].ndim - 1)
    axis = parts[0].ndim - 1
    low = (lane // 32) % 2 == 0
    high = lane < 64

    def swap(first, second, width, mask):
        return (
            jnp.where(mask, first, pltpu.roll(second, width, axis)),
            jnp.where(mask, pltpu.roll(first, 128 - width, axis), second),
        )

    p0, p1 = swap(parts[0], parts[1], 32, low)
    p2, p3 = swap(parts[2], parts[3], 32, low)
    p0, p2 = swap(p0, p2, 64, high)
    p1, p3 = swap(p1, p3, 64, high)
    return p0, p1, p2, p3


def turn(parts, sign):
    (r0, i0), (r1, i1), (r2, i2), (r3, i3) = parts
    er, ei, fr, fi = r0 + r2, i0 + i2, r0 - r2, i0 - i2
    gr, gi, hr, hi = r1 + r3, i1 + i3, r1 - r3, i1 - i3
    if sign < 0:
        hr, hi = -hr, -hi
    return (
        (er + gr, ei + gi),
        (fr - hi, fi + hr),
        (er - gr, ei - gi),
        (fr + hi, fi - hr),
    )


def waves_of(first_row):
    along_y = (first_row + lax.broadcasted_iota(jnp.int32, (ROWS, NG), 0)).astype(F32)
    index = lax.broadcasted_iota(jnp.int32, (ROWS, NG), 1)
    along_x = jnp.where(index < NG // 2, index, index - NG).astype(F32)
    return along_y, along_x


def columns_kernel(row_ref, re_ref, im_ref, table_ref, out_ref, left_ref, prod_ref, turn_ref):
    along_y, along_x = waves_of(row_ref[0])
    wave_sq = along_y * along_y + along_x * along_x
    inverse = jnp.where(wave_sq > 0.5, 1.0 / jnp.maximum(wave_sq, 1.0), 0.0)
    scale_y = along_y * inverse
    scale_x = along_x * inverse
    for mode in range(OWN):
        w_re, w_im = re_ref[mode], im_ref[mode]
        fields = (
            (w_re, w_im),
            (-scale_y * w_im, scale_y * w_re),
            (scale_x * w_im, -scale_x * w_re),
        )
        for member, (f_re, f_im) in enumerate(fields):
            pieces = [
                (f_re[:, QUART * p : QUART * (p + 1)], f_im[:, QUART * p : QUART * (p + 1)])
                for p in range(4)
            ]
            at = (member * OWN + mode) * ROWS
            for part, (b_re, b_im) in enumerate(turn(pieces, 1)):
                left_ref[part, at : at + ROWS, :QUART] = b_re.astype(BF)
                left_ref[part, at : at + ROWS, QUART:] = b_im.astype(BF)
    for part in range(PARTS):
        prod_ref[part] = (
            jnp.dot(left_ref[part], table_ref[part], preferred_element_type=F32) * FACTOR
        )
    count = 3 * OWN
    for at in range(count):
        rows = slice(at * ROWS, (at + 1) * ROWS)
        block = jnp.concatenate(
            [prod_ref[part, rows, c * QUART : (c + 1) * QUART] for part in range(PARTS) for c in range(2)],
            axis=0,
        )
        turn_ref[pl.ds(at, DEVS, stride=24), :] = block.T
    out_ref[...] = turn_ref[...].reshape(DEVS, 24, 128)[:, :count].astype(BF)


def points_kernel(in_ref, ahead_ref, triple_ref, back_ref, out_ref, left_ref, phys_ref, flux_ref, half_ref):
    count = 3 * OWN
    tall = 24 * GROUPS
    chunk = 256

    def gather(pair, carry):
        for quad in range(SLABS // 4):
            sides = []
            for side in range(2):
                group = pair * 2 + side
                parts = []
                for j in range(4):
                    block = in_ref[group, quad, j].astype(F32)
                    parts.append(jnp.concatenate([block, jnp.zeros((24 - count, 128), F32)], axis=0))
                sides.append(regroup(parts))
            for part in range(PARTS):
                both = jnp.concatenate([sides[0][part], sides[1][part]], axis=0)
                left_ref[part, pl.ds(pl.multiple_of(pair * 48, 48), 48), quad * 128 : (quad + 1) * 128] = both.astype(BF)
        return carry

    lax.fori_loop(0, GROUPS // 2, gather, 0)
    flux_ref[...] = jnp.zeros_like(flux_ref)

    def line(part, carry):
        phys_ref[...] = jnp.dot(left_ref[part], ahead_ref[...], preferred_element_type=F32) * FACTOR

        def points(step, inner):
            lanes = pl.ds(pl.multiple_of(step * chunk, chunk), chunk)
            right = phys_ref[:, lanes].astype(BF)
            sum_x = jnp.zeros((MODES, chunk), F32)
            sum_y = jnp.zeros((MODES, chunk), F32)
            for group in range(GROUPS):
                made = jnp.dot(
                    triple_ref[group * OWN * MODES : (group + 1) * OWN * MODES, :],
                    right,
                    preferred_element_type=F32,
                )
                vel = phys_ref[group * 24 : (group + 1) * 24, lanes]
                for mode in range(OWN):
                    block = made[mode * MODES : (mode + 1) * MODES]
                    sum_x = sum_x + block * vel[OWN + mode : OWN + mode + 1]
                    sum_y = sum_y + block * vel[2 * OWN + mode : 2 * OWN + mode + 1]
            for group in range(GROUPS):
                at = group * 16
                flux_ref[at : at + OWN, lanes] = sum_x[group * OWN : (group + 1) * OWN]
                flux_ref[at + OWN : at + 2 * OWN, lanes] = sum_y[group * OWN : (group + 1) * OWN]
            return inner

        lax.fori_loop(0, NG // chunk, points, 0)
        half_ref[part] = jnp.dot(flux_ref[...].astype(BF), back_ref[...], preferred_element_type=F32) * FACTOR
        return carry

    lax.fori_loop(0, PARTS, line, 0)
    for quad in range(LIVE // 4):
        parts = regroup([half_ref[part, :, quad * 128 : (quad + 1) * 128] for part in range(PARTS)])
        for j in range(4):
            block = parts[j].astype(BF)
            for group in range(GROUPS):
                out_ref[group, quad * 4 + j] = block[group * 16 : (group + 1) * 16]
    out_ref[:, LIVE:] = jnp.zeros((GROUPS, SLABS - LIVE, 16, 128), BF)


def update_kernel(
    row_ref, in_ref, table_ref, re_ref, im_ref, base_re_ref, base_im_ref, new_re_ref, new_im_ref, wide_ref, left_ref, prod_ref
):
    wide_ref[...] = in_ref[...].astype(F32).reshape(DEVS * 16, 128)
    for at in range(2 * OWN):
        block = wide_ref[pl.ds(at, DEVS, stride=16), :].T.astype(BF)
        for part in range(PARTS):
            for c in range(2):
                row = (part * 2 + c) * ROWS
                left_ref[part, at * ROWS : (at + 1) * ROWS, c * QUART : (c + 1) * QUART] = block[row : row + ROWS]
    for part in range(PARTS):
        prod_ref[part] = (
            jnp.dot(left_ref[part], table_ref[part], preferred_element_type=F32) * FACTOR
        )
    along_y, along_x = waves_of(row_ref[0])
    wave_sq = along_y * along_y + along_x * along_x
    keep = (jnp.abs(along_x) * 3.0 < NG) & (along_y * 3.0 < NG)
    damping = VISCOSITY / (NG * NG) * wave_sq
    for mode in range(OWN):
        spectra = []
        for member in range(2):
            rows = slice((member * OWN + mode) * ROWS, (member * OWN + mode + 1) * ROWS)
            spectra.append(
                turn([(prod_ref[part, rows, :QUART], prod_ref[part, rows, QUART:]) for part in range(PARTS)], -1)
            )
        for p in range(4):
            lanes = slice(p * QUART, (p + 1) * QUART)
            (x_re, x_im), (y_re, y_im) = spectra[0][p], spectra[1][p]
            wx, wy = along_x[:, lanes], along_y[:, lanes]
            adv_re = jnp.where(keep[:, lanes], -(wx * x_im + wy * y_im), 0.0)
            adv_im = jnp.where(keep[:, lanes], wx * x_re + wy * y_re, 0.0)
            damp = damping[:, lanes]
            new_re_ref[mode, :, lanes] = base_re_ref[mode, :, lanes] + STEP_WEIGHT * (
                -adv_re - damp * re_ref[mode, :, lanes]
            )
            new_im_ref[mode, :, lanes] = base_im_ref[mode, :, lanes] + STEP_WEIGHT * (
                -adv_im - damp * im_ref[mode, :, lanes]
            )


def call(kernel, outs, scratch, specs, flops):
    return pl.pallas_call(
        kernel,
        out_shape=outs,
        in_specs=specs,
        out_specs=jax.tree.map(lambda _: pl.BlockSpec(memory_space=pltpu.VMEM), outs),
        scratch_shapes=scratch,
        cost_estimate=pl.CostEstimate(flops=flops, bytes_accessed=4 * 1024 * 1024, transcendentals=0),
        compiler_params=pltpu.CompilerParams(vmem_limit_bytes=VMEM_LIMIT),
    )


def shards(omega_re, omega_im, base_re, base_im, triple):
    vmem = pl.BlockSpec(memory_space=pltpu.VMEM)
    smem = pl.BlockSpec(memory_space=pltpu.SMEM)
    count = 3 * OWN
    ahead_x, back_x = x_tables()
    ahead_y, back_y = y_tables()
    first_row = (lax.axis_index("grid") * ROWS).astype(jnp.int32)[None]
    spread = np.zeros((MODES, 24 * GROUPS), np.float32)
    for mode in range(MODES):
        spread[mode, (mode // OWN) * 24 + mode % OWN] = 1.0
    wide_triple = jnp.dot(
        triple.reshape(MODES * MODES, MODES), spread.astype(ml_dtypes.bfloat16), preferred_element_type=BF
    )
    columns = call(
        columns_kernel,
        jax.ShapeDtypeStruct((DEVS, count, 128), BF),
        [
            pltpu.VMEM((PARTS, count * ROWS, 2 * QUART), BF),
            pltpu.VMEM((PARTS, count * ROWS, 2 * QUART), F32),
            pltpu.VMEM((DEVS * 24, 128), F32),
        ],
        [smem, vmem, vmem, vmem],
        1_000_000_000,
    )(first_row, omega_re, omega_im, ahead_x)
    slab = lax.all_to_all(columns, ("mode", "grid"), split_axis=0, concat_axis=0, tiled=True)
    halves = call(
        points_kernel,
        jax.ShapeDtypeStruct((GROUPS, SLABS, 16, 128), BF),
        [
            pltpu.VMEM((PARTS, 24 * GROUPS, NG), BF),
            pltpu.VMEM((24 * GROUPS, NG), F32),
            pltpu.VMEM((16 * GROUPS, NG), F32),
            pltpu.VMEM((PARTS, 16 * GROUPS, LIVE * 32), F32),
        ],
        [vmem] * 4,
        10_000_000_000,
    )(slab.reshape(GROUPS, SLABS // 4, 4, count, 128), ahead_y, wide_triple, back_y)
    rows = lax.all_to_all(halves.reshape(DEVS, 16, 128), ("mode", "grid"), split_axis=0, concat_axis=0, tiled=True)
    new = jax.ShapeDtypeStruct(base_re.shape, F32)
    return call(
        update_kernel,
        (new, new),
        [
            pltpu.VMEM((DEVS * 16, 128), F32),
            pltpu.VMEM((PARTS, 2 * OWN * ROWS, 2 * QUART), BF),
            pltpu.VMEM((PARTS, 2 * OWN * ROWS, 2 * QUART), F32),
        ],
        [smem] + [vmem] * 6,
        1_000_000_000,
    )(first_row, rows, back_x, omega_re, omega_im, base_re, base_im)


def solution(mesh):
    spec = P("mode", "grid", None)
    return jax.shard_map(
        shards, mesh=mesh, in_specs=(spec, spec, spec, spec, P()), out_specs=(spec, spec), check_vma=False
    )
```

profile of v0, /device:TPU:1, one launch (start us, length us, event | category | flops | bytes accessed | tf_op | source)
XLA Modules:
  0.0 130.8 jit_solution(15746588495734437673)
XLA Ops:
  0.6 0.0 copy-start
  0.6 5.1 %shard_map.113 = bf16[256,21,128]{2,1,0:T(8,128)(2,1)} custom-call(s32[1]{0:T(128)} %bitcast.row_ref, f32[7,16,1024]{2,1,0:T(8,128)} %re_ref.3, f32[7,16,1024]{2,1,0:T(8,128)} %im_ref.3, bf16[4,512,512]{2,1,0:T(8,128)(2,1)} %constant.17.clone.table_ref), custom_call_target="tpu_custom_call" | custom-call | flops 1000000000 | bytes 4194304 | tf_op jit(solution)/shard_map/pallas_call | solution.py:268
  5.8 0.0 copy-start.2
  5.8 15.7 %all-to-all-start = ((bf16[256,21,128]{2,1,0:T(8,128)(2,1)}), bf16[256,21,128]{2,1,0:T(8,128)(2,1)S(1)}, u32[]{:S(2)}, u32[]{:S(2)}) async-start(bf16[256,21,128]{2,1,0:T(8,128)(2,1)} %shard_map.113), calls=%async_computation | async-start | bytes 3145728 | tf_op jit(solution)/shard_map/all_to_all | solution.py:279
  21.4 0.0 copy-done
  21.4 0.0 copy-done.2
  21.4 1.7 %convolution_bitcast_fusion.triple_ref = bf16[3136,192]{1,0:T(8,128)(2,1)} fusion(bf16[56,192]{1,0:T(8,128)(2,1)S(1)} %copy-done.2, bf16[3136,56]{1,0:T(8,128)(2,1)S(1)} %bitcast.8), kind=kOutput, calls=%fused_computation | convolution fusion | flops 67436544 | bytes 1576960 | tf_op jit(solution)/shard_map/dot_general | solution.py:265
  23.2 40.5 %all-to-all-done = bf16[256,21,128]{2,1,0:T(8,128)(2,1)S(1)} async-done(((bf16[256,21,128]{2,1,0:T(8,128)(2,1)}), bf16[256,21,128]{2,1,0:T(8,128)(2,1)S(1)}, u32[]{:S(2)}, u32[]{:S(2)}) %all-to-all-start) | async-done | bytes 1376288 | tf_op jit(solution)/shard_map/all_to_all | solution.py:279
  63.7 0.0 copy-start.1
  63.7 1.2 copy-done.1
  64.8 23.5 %shard_map.114 = bf16[8,32,16,128]{3,2,1,0:T(8,128)(2,1)} custom-call(bf16[8,8,4,21,128]{4,3,2,1,0:T(8,128)(2,1)} %bitcast.9, bf16[1024,1024]{1,0:T(8,128)(2,1)} %constant.18.clone.ahead_ref, bf16[3136,192]{1,0:T(8,128)(2,1)} %convolution_bitcast_fusion.triple_ref, bf16[1024,768]{1,0:T(8,128)(2,1)} %constant.19.clone.back_ref), custom_call_target="tpu_custom_call" | custom-call | flops 10000000000 | bytes 4194304 | tf_op jit(solution)/shard_map/pallas_call | solution.py:280
  88.3 37.5 %all_to_all.10.in_ref = bf16[256,16,128]{2,1,0:T(8,128)(2,1)} all-to-all(bf16[256,16,128]{2,1,0:T(8,128)(2,1)} %bitcast.10), channel_id=1, replica_groups=mesh['mode'=8,'grid'=32] {'mode','grid'}, dimensions={0} | all-to-all | bytes 2097152 | tf_op jit(solution)/shard_map/all_to_all | solution.py:292
  125.8 5.0 %shard_map.115 = (f32[7,16,1024]{2,1,0:T(8,128)}, f32[7,16,1024]{2,1,0:T(8,128)}) custom-call(s32[1]{0:T(128)} %bitcast.row_ref, bf16[256,16,128]{2,1,0:T(8,128)(2,1)} %all_to_all.10.in_ref, bf16[4,512,512]{2,1,0:T(8,128)(2,1)} %constant.20.clone.table_ref, f32[7,16,1024]{2,1,0:T(8,128)} %re_ref.3, f32[7,16,1024]{2,1,0:T(8,128)} %im_ref.3, ...), custom_call_target="tpu_custom_call" | custom-call | flops 1000000000 | bytes 4194304 | tf_op jit(solution)/shard_map/pallas_call | solution.py:294
Async XLA Ops:
  0.6 20.8 %copy-start = (bf16[56,56,56]{2,1,0:T(8,128)(2,1)S(1)}, bf16[56,56,56]{2,1,0:T(8,128)(2,1)}, u32[]{:S(2)}) copy-start(bf16[56,56,56]{2,1,0:T(8,128)(2,1)} %param.14) | copy-start | bytes 1053700
  5.8 15.7 %copy-start.2 = (bf16[56,192]{1,0:T(8,128)(2,1)S(1)}, bf16[56,192]{1,0:T(8,128)(2,1)}, u32[]{:S(2)}) copy-start(bf16[56,192]{1,0:T(8,128)(2,1)} %constant.16.clone) | copy-start | bytes 64516
  5.8 57.9 %all-to-all-start = ((bf16[256,21,128]{2,1,0:T(8,128)(2,1)}), bf16[256,21,128]{2,1,0:T(8,128)(2,1)S(1)}, u32[]{:S(2)}, u32[]{:S(2)}) async-start(bf16[256,21,128]{2,1,0:T(8,128)(2,1)} %shard_map.113), calls=%async_computation | async-start | bytes 3145728 | tf_op jit(solution)/shard_map/all_to_all | solution.py:279
  63.7 1.2 copy-start.1
where the time goes:
time: 131 us
  waiting for transfers between devices  40.5 us (31%)
  blocking collectives  37.5 us (29%)
  Pallas kernels  33.6 us (26%)
  starting transfers between devices  15.7 us (12%)
  matrix products  1.72 us (1%)
    all_to_all x1, waiting for transfers between devices, shards(): lax.all_to_all(columns, ('mode', 'grid'), split_axis=0, concat_axis=0, ti...  40.5 us
    all_to_all x1, blocking collectives, shards(): lax.all_to_all(halves.reshape(DEVS, 16, 128), ('mode', 'grid'), split_axi...  37.5 us
    pallas_call x1, Pallas kernels, shards(): call(points_kernel, jax.ShapeDtypeStruct((GROUPS, SLABS, 16, 128), BF), [...  23.5 us
    all_to_all x1, starting transfers between devices, shards(): lax.all_to_all(columns, ('mode', 'grid'), split_axis=0, concat_axis=0, ti...  15.7 us
    pallas_call x1, Pallas kernels, shards(): call(columns_kernel, jax.ShapeDtypeStruct((DEVS, count, 128), BF), [pltpu...  5.11 us
    pallas_call x1, Pallas kernels, shards(): call(update_kernel, (new, new), [pltpu.VMEM((DEVS * 16, 128), F32), pltpu...  5.04 us
  transfers between devices with their start and end apart: 1, of which 1 were waited for; matrix products, arithmetic and copies ran while one was open for 1% of the time, Pallas kernels for 0%

commit v1 on v0

--- a/solution.py
+++ b/solution.py
@@ -26,7 +26,7 @@
 LIVE = 24
 BF = jnp.bfloat16
 F32 = jnp.float32
-VMEM_LIMIT = 56 * 1024 * 1024
+VMEM_LIMIT = 20 * 1024 * 1024
 
 
 def circle(phases):
@@ -141,7 +141,7 @@
 def points_kernel(in_ref, ahead_ref, triple_ref, back_ref, out_ref, left_ref, phys_ref, flux_ref, half_ref):
     count = 3 * OWN
     tall = 24 * GROUPS
-    chunk = 256
+    chunk = 512
 
     def gather(pair, carry):
         for quad in range(SLABS // 4):

time: 131 us -> 127 us (0.969)
  Pallas kernels: 33.6 us -> 24.5 us
  local copies, waits for them, and re-layouts: 1.17 us -> 6.73 us
    unnamed x6 -> x24, local copies, waits for them, and re-layouts: 1.17 us -> 6.73 us
    pallas_call x1, Pallas kernels: 23.5 us -> 18.5 us  [shards(): call(points_kernel, jax.ShapeDtypeStruct((GROUPS, SLABS, 16, 128), BF), [...]
    pallas_call x1, Pallas kernels: 5.04 us -> 2.74 us  [shards(): call(update_kernel, (new, new), [pltpu.VMEM((DEVS * 16, 128), F32), pltpu...]
    pallas_call x1, Pallas kernels: 5.11 us -> 3.26 us  [shards(): call(columns_kernel, jax.ShapeDtypeStruct((DEVS, count, 128), BF), [pltpu...]
  transfers between devices with their start and end apart: 1 -> 1, of which waited for: 1 -> 1; matrix products, arithmetic and copies ran while one was open for 1% -> 0% of each run, Pallas kernels for 0% -> 0%
where the time goes in v1:
time: 127 us
  waiting for transfers between devices  40.9 us (32%)
  blocking collectives  37.2 us (29%)
  Pallas kernels  24.5 us (19%)
  starting transfers between devices  16.5 us (13%)
  local copies, waits for them, and re-layouts  6.73 us (5%)
    all_to_all x1, waiting for transfers between devices, shards(): lax.all_to_all(columns, ('mode', 'grid'), split_axis=0, concat_axis=0, ti...  40.9 us
    all_to_all x1, blocking collectives, shards(): lax.all_to_all(halves.reshape(DEVS, 16, 128), ('mode', 'grid'), split_axi...  37.2 us
    pallas_call x1, Pallas kernels, shards(): call(points_kernel, jax.ShapeDtypeStruct((GROUPS, SLABS, 16, 128), BF), [...  18.5 us
    all_to_all x1, starting transfers between devices, shards(): lax.all_to_all(columns, ('mode', 'grid'), split_axis=0, concat_axis=0, ti...  16.5 us
    unnamed x24, local copies, waits for them, and re-layouts  6.73 us
    pallas_call x1, Pallas kernels, shards(): call(columns_kernel, jax.ShapeDtypeStruct((DEVS, count, 128), BF), [pltpu...  3.26 us
    pallas_call x1, Pallas kernels, shards(): call(update_kernel, (new, new), [pltpu.VMEM((DEVS * 16, 128), F32), pltpu...  2.74 us
  transfers between devices with their start and end apart: 1, of which 1 were waited for; matrix products, arithmetic and copies ran while one was open for 0% of the time, Pallas kernels for 0%

profile of v1, /device:TPU:1, one launch (start us, length us, event | category | flops | bytes accessed | tf_op | source)
XLA Modules:
  0.0 127.1 jit_solution(8897266047755152718)
XLA Ops:
  0.6 0.0 copy-start
  0.6 0.0 copy-start.1
  0.7 1.7 %copy-done.1 = bf16[4,512,512]{2,1,0:T(8,128)(2,1)S(1)} copy-done((bf16[4,512,512]{2,1,0:T(8,128)(2,1)S(1)}, bf16[4,512,512]{2,1,0:T(8,128)(2,1)}, u32[]{:S(2)}) %copy-start.1) | copy-done | bytes 2097176
  2.3 0.0 copy-start.3
  2.3 1.0 copy-done.3
  3.3 0.0 copy-start.5
  3.3 1.0 copy-done.5
  4.4 3.3 %shard_map.113 = bf16[256,21,128]{2,1,0:T(8,128)(2,1)} custom-call(s32[1]{0:T(128)} %bitcast.row_ref, f32[7,16,1024]{2,1,0:T(8,128)S(1)} %copy-done.3, f32[7,16,1024]{2,1,0:T(8,128)S(1)} %copy-done.5, bf16[4,512,512]{2,1,0:T(8,128)(2,1)S(1)} %copy-done.1), custom_call_target="tpu_custom_call" | custom-call | flops 1000000000 | bytes 4194304 | tf_op jit(solution)/shard_map/pallas_call | solution.py:268
  7.6 0.0 copy-start.11
  7.6 16.5 %all-to-all-start = ((bf16[256,21,128]{2,1,0:T(8,128)(2,1)}), bf16[256,21,128]{2,1,0:T(8,128)(2,1)}, u32[]{:S(2)}, u32[]{:S(2)}) async-start(bf16[256,21,128]{2,1,0:T(8,128)(2,1)} %shard_map.113), calls=%async_computation | async-start | bytes 3145728 | tf_op jit(solution)/shard_map/all_to_all | solution.py:279
  24.2 0.0 copy-done
  24.2 0.0 copy-done.11
  24.2 0.5 convolution_bitcast_fusion.triple_ref
  24.7 40.9 %all-to-all-done = bf16[256,21,128]{2,1,0:T(8,128)(2,1)} async-done(((bf16[256,21,128]{2,1,0:T(8,128)(2,1)}), bf16[256,21,128]{2,1,0:T(8,128)(2,1)}, u32[]{:S(2)}, u32[]{:S(2)}) %all-to-all-start) | async-done | bytes 1376288 | tf_op jit(solution)/shard_map/all_to_all | solution.py:279
  65.6 0.0 copy-start.9
  65.6 1.6 %copy-done.9 = bf16[1024,1024]{1,0:T(8,128)(2,1)S(1)} copy-done((bf16[1024,1024]{1,0:T(8,128)(2,1)S(1)}, bf16[1024,1024]{1,0:T(8,128)(2,1)}, u32[]{:S(2)}) %copy-start.9) | copy-done | bytes 2097176
  67.2 0.0 copy-start.10
  67.2 1.4 %copy-done.10 = bf16[1024,768]{1,0:T(8,128)(2,1)S(1)} copy-done((bf16[1024,768]{1,0:T(8,128)(2,1)S(1)}, bf16[1024,768]{1,0:T(8,128)(2,1)}, u32[]{:S(2)}) %copy-start.10) | copy-done | bytes 1572888
  68.6 0.0 copy-start.4
  68.6 0.0 copy-start.6
  68.6 0.0 copy-start.7
  68.6 0.0 copy-start.8
  68.6 18.5 %shard_map.114 = bf16[8,32,16,128]{3,2,1,0:T(8,128)(2,1)S(1)} custom-call(bf16[8,8,4,21,128]{4,3,2,1,0:T(8,128)(2,1)} %bitcast.1.in_ref, bf16[1024,1024]{1,0:T(8,128)(2,1)S(1)} %copy-done.9, bf16[3136,192]{1,0:T(8,128)(2,1)S(1)} %convolution_bitcast_fusion.triple_ref, bf16[1024,768]{1,0:T(8,128)(2,1)S(1)} %copy-done.10), custom_call_target="tpu_custom_call" | custom-call | flops 10000000000 | bytes 4194304 | tf_op jit(solution)/shard_map/pallas_call | solution.py:280
  87.1 0.0 copy-start.2
  87.1 37.2 %all_to_all.10.in_ref = bf16[256,16,128]{2,1,0:T(8,128)(2,1)S(1)} all-to-all(bf16[256,16,128]{2,1,0:T(8,128)(2,1)S(1)} %bitcast.9), channel_id=1, replica_groups=mesh['mode'=8,'grid'=32] {'mode','grid'}, dimensions={0} | all-to-all | bytes 2097152 | tf_op jit(solution)/shard_map/all_to_all | solution.py:292
  124.3 0.0 copy-done.4
  124.3 0.0 copy-done.6
  124.3 0.0 copy-done.7
  124.3 0.0 copy-done.8
  124.3 0.0 copy-done.2
  124.3 2.7 %shard_map.115 = (f32[7,16,1024]{2,1,0:T(8,128)}, f32[7,16,1024]{2,1,0:T(8,128)}) custom-call(s32[1]{0:T(128)} %bitcast.row_ref, bf16[256,16,128]{2,1,0:T(8,128)(2,1)S(1)} %all_to_all.10.in_ref, bf16[4,512,512]{2,1,0:T(8,128)(2,1)S(1)} %copy-done.2, f32[7,16,1024]{2,1,0:T(8,128)S(1)} %copy-done.4, f32[7,16,1024]{2,1,0:T(8,128)S(1)} %copy-done.6, ...), custom_call_target="tpu_custom_call" | custom-call | flops 1000000000 | bytes 4194304 | tf_op jit(solution)/shard_map/pallas_call | solution.py:294
Async XLA Ops:
  0.6 23.5 %copy-start = (bf16[56,56,56]{2,1,0:T(8,128)(2,1)S(1)}, bf16[56,56,56]{2,1,0:T(8,128)(2,1)}, u32[]{:S(2)}) copy-start(bf16[56,56,56]{2,1,0:T(8,128)(2,1)} %param.14) | copy-start | bytes 1053700
  0.6 1.7 %copy-start.1 = (bf16[4,512,512]{2,1,0:T(8,128)(2,1)S(1)}, bf16[4,512,512]{2,1,0:T(8,128)(2,1)}, u32[]{:S(2)}) copy-start(bf16[4,512,512]{2,1,0:T(8,128)(2,1)} %constant.17.clone.table_ref) | copy-start | bytes 6291460
  2.3 1.0 copy-start.3
  3.3 1.0 copy-start.5
  7.6 16.6 %copy-start.11 = (bf16[56,192]{1,0:T(8,128)(2,1)S(1)}, bf16[56,192]{1,0:T(8,128)(2,1)}, u32[]{:S(2)}) copy-start(bf16[56,192]{1,0:T(8,128)(2,1)} %constant.16.clone) | copy-start | bytes 64516
  7.6 58.0 %all-to-all-start = ((bf16[256,21,128]{2,1,0:T(8,128)(2,1)}), bf16[256,21,128]{2,1,0:T(8,128)(2,1)}, u32[]{:S(2)}, u32[]{:S(2)}) async-start(bf16[256,21,128]{2,1,0:T(8,128)(2,1)} %shard_map.113), calls=%async_computation | async-start | bytes 3145728 | tf_op jit(solution)/shard_map/all_to_all | solution.py:279
  65.6 1.6 %copy-start.9 = (bf16[1024,1024]{1,0:T(8,128)(2,1)S(1)}, bf16[1024,1024]{1,0:T(8,128)(2,1)}, u32[]{:S(2)}) copy-start(bf16[1024,1024]{1,0:T(8,128)(2,1)} %constant.18.clone.ahead_ref) | copy-start | bytes 6291460
  67.2 1.4 %copy-start.10 = (bf16[1024,768]{1,0:T(8,128)(2,1)S(1)}, bf16[1024,768]{1,0:T(8,128)(2,1)}, u32[]{:S(2)}) copy-start(bf16[1024,768]{1,0:T(8,128)(2,1)} %constant.19.clone.back_ref) | copy-start | bytes 4718596
  68.6 55.7 %copy-start.4 = (f32[7,16,1024]{2,1,0:T(8,128)S(1)}, f32[7,16,1024]{2,1,0:T(8,128)}, u32[]{:S(2)}) copy-start(f32[7,16,1024]{2,1,0:T(8,128)} %re_ref.3) | copy-start | bytes 1376260
  68.6 55.7 %copy-start.6 = (f32[7,16,1024]{2,1,0:T(8,128)S(1)}, f32[7,16,1024]{2,1,0:T(8,128)}, u32[]{:S(2)}) copy-start(f32[7,16,1024]{2,1,0:T(8,128)} %im_ref.3) | copy-start | bytes 1376260
  68.6 55.7 %copy-start.7 = (f32[7,16,1024]{2,1,0:T(8,128)S(1)}, f32[7,16,1024]{2,1,0:T(8,128)}, u32[]{:S(2)}) copy-start(f32[7,16,1024]{2,1,0:T(8,128)} %base_re_ref.1) | copy-start | bytes 1376260
  68.6 55.7 %copy-start.8 = (f32[7,16,1024]{2,1,0:T(8,128)S(1)}, f32[7,16,1024]{2,1,0:T(8,128)}, u32[]{:S(2)}) copy-start(f32[7,16,1024]{2,1,0:T(8,128)} %base_im_ref.1) | copy-start | bytes 1376260
  87.1 37.2 %copy-start.2 = (bf16[4,512,512]{2,1,0:T(8,128)(2,1)S(1)}, bf16[4,512,512]{2,1,0:T(8,128)(2,1)}, u32[]{:S(2)}) copy-start(bf16[4,512,512]{2,1,0:T(8,128)(2,1)} %constant.20.clone.table_ref) | copy-start | bytes 6291460

commit v2 on v1

--- a/solution.py
+++ b/solution.py
@@ -26,7 +26,8 @@
 LIVE = 24
 BF = jnp.bfloat16
 F32 = jnp.float32
-VMEM_LIMIT = 20 * 1024 * 1024
+SMALL = 20 * 1024 * 1024
+LARGE = 56 * 1024 * 1024
 
 
 def circle(phases):
@@ -61,23 +62,15 @@
     return ahead, back
 
 
-def regroup(parts):
-    lane = lax.broadcasted_iota(jnp.int32, parts[0].shape, parts[0].ndim - 1)
-    axis = parts[0].ndim - 1
-    low = (lane // 32) % 2 == 0
-    high = lane < 64
-
-    def swap(first, second, width, mask):
-        return (
-            jnp.where(mask, first, pltpu.roll(second, width, axis)),
-            jnp.where(mask, pltpu.roll(first, 128 - width, axis), second),
-        )
-
-    p0, p1 = swap(parts[0], parts[1], 32, low)
-    p2, p3 = swap(parts[2], parts[3], 32, low)
-    p0, p2 = swap(p0, p2, 64, high)
-    p1, p3 = swap(p1, p3, 64, high)
-    return p0, p1, p2, p3
+def lane_masks():
+    group = lax.broadcasted_iota(jnp.int32, (1, 128), 1) // 32
+    return [group == 0, group == 1, group == 2]
+
+
+def pick(masks, sources):
+    return jnp.where(
+        masks[0], sources[0], jnp.where(masks[1], sources[1], jnp.where(masks[2], sources[2], sources[3]))
+    )
 
 
 def turn(parts, sign):
@@ -101,13 +94,36 @@
     return along_y, along_x
 
 
-def columns_kernel(row_ref, re_ref, im_ref, table_ref, out_ref, left_ref, prod_ref, turn_ref):
+def columns_kernel(
+    row_ref, re_hbm, im_hbm, table_hbm, out_ref, re_ref, im_ref, table_ref, left_ref, prod_ref, turn_ref, sems
+):
+    loads = []
+    for mode in range(OWN):
+        loads.append(
+            (
+                pltpu.make_async_copy(re_hbm.at[mode], re_ref.at[mode], sems.at[2 * mode]),
+                pltpu.make_async_copy(im_hbm.at[mode], im_ref.at[mode], sems.at[2 * mode + 1]),
+            )
+        )
+    tables = [
+        pltpu.make_async_copy(table_hbm.at[part], table_ref.at[part], sems.at[2 * OWN + part]) for part in range(PARTS)
+    ]
+    for pair in loads:
+        pair[0].start()
+        pair[1].start()
+    for copy in tables:
+        copy.start()
+    count = 3 * OWN
+    for at in range(count, 24):
+        turn_ref[pl.ds(at, DEVS, stride=24), :] = jnp.zeros((DEVS, 128), F32)
     along_y, along_x = waves_of(row_ref[0])
     wave_sq = along_y * along_y + along_x * along_x
     inverse = jnp.where(wave_sq > 0.5, 1.0 / jnp.maximum(wave_sq, 1.0), 0.0)
     scale_y = along_y * inverse
     scale_x = along_x * inverse
     for mode in range(OWN):
+        loads[mode][0].wait()
+        loads[mode][1].wait()
         w_re, w_im = re_ref[mode], im_ref[mode]
         fields = (
             (w_re, w_im),
@@ -124,35 +140,44 @@
                 left_ref[part, at : at + ROWS, :QUART] = b_re.astype(BF)
                 left_ref[part, at : at + ROWS, QUART:] = b_im.astype(BF)
     for part in range(PARTS):
+        tables[part].wait()
         prod_ref[part] = (
             jnp.dot(left_ref[part], table_ref[part], preferred_element_type=F32) * FACTOR
         )
-    count = 3 * OWN
+    shift = row_ref[1]
+    slots = [lax.rem(slot + PARTS - shift, PARTS) for slot in range(PARTS)]
     for at in range(count):
         rows = slice(at * ROWS, (at + 1) * ROWS)
         block = jnp.concatenate(
-            [prod_ref[part, rows, c * QUART : (c + 1) * QUART] for part in range(PARTS) for c in range(2)],
+            [prod_ref[slots[slot], rows, c * QUART : (c + 1) * QUART] for slot in range(PARTS) for c in range(2)],
             axis=0,
         )
         turn_ref[pl.ds(at, DEVS, stride=24), :] = block.T
-    out_ref[...] = turn_ref[...].reshape(DEVS, 24, 128)[:, :count].astype(BF)
-
-
-def points_kernel(in_ref, ahead_ref, triple_ref, back_ref, out_ref, left_ref, phys_ref, flux_ref, half_ref):
-    count = 3 * OWN
-    tall = 24 * GROUPS
+    out_ref[...] = turn_ref[...].reshape(DEVS, 24, 128).astype(BF)
+
+
+def points_kernel(
+    in_ref, ahead_hbm, triple_hbm, back_hbm, out_ref, ahead_ref, triple_ref, back_ref, left_ref, phys_ref, flux_ref, half_ref, sems
+):
     chunk = 512
+    ahead = pltpu.make_async_copy(ahead_hbm, ahead_ref, sems.at[0])
+    couple = pltpu.make_async_copy(triple_hbm, triple_ref, sems.at[1])
+    back = pltpu.make_async_copy(back_hbm, back_ref, sems.at[2])
+    ahead.start()
+    couple.start()
+    back.start()
+    masks = lane_masks()
 
     def gather(pair, carry):
         for quad in range(SLABS // 4):
             sides = []
             for side in range(2):
-                group = pair * 2 + side
+                blocks = [in_ref[pair * 2 + side, quad, j].astype(F32) for j in range(4)]
                 parts = []
-                for j in range(4):
-                    block = in_ref[group, quad, j].astype(F32)
-                    parts.append(jnp.concatenate([block, jnp.zeros((24 - count, 128), F32)], axis=0))
-                sides.append(regroup(parts))
+                for part in range(PARTS):
+                    mixed = pick(masks, [blocks[(slot - part) % 4] for slot in range(4)])
+                    parts.append(pltpu.roll(mixed, 128 - 32 * part, 1) if part else mixed)
+                sides.append(parts)
             for part in range(PARTS):
                 both = jnp.concatenate([sides[0][part], sides[1][part]], axis=0)
                 left_ref[part, pl.ds(pl.multiple_of(pair * 48, 48), 48), quad * 128 : (quad + 1) * 128] = both.astype(BF)
@@ -160,13 +185,17 @@
 
     lax.fori_loop(0, GROUPS // 2, gather, 0)
     flux_ref[...] = jnp.zeros_like(flux_ref)
+    ahead.wait()
+    couple.wait()
+    back.wait()
 
     def line(part, carry):
         phys_ref[...] = jnp.dot(left_ref[part], ahead_ref[...], preferred_element_type=F32) * FACTOR
-
-        def points(step, inner):
-            lanes = pl.ds(pl.multiple_of(step * chunk, chunk), chunk)
-            right = phys_ref[:, lanes].astype(BF)
+        for step in range(NG // chunk):
+            lanes = slice(step * chunk, (step + 1) * chunk)
+            right = jnp.concatenate(
+                [phys_ref[group * 24 : group * 24 + OWN, lanes] for group in range(GROUPS)], axis=0
+            ).astype(BF)
             sum_x = jnp.zeros((MODES, chunk), F32)
             sum_y = jnp.zeros((MODES, chunk), F32)
             for group in range(GROUPS):
@@ -184,17 +213,17 @@
                 at = group * 16
                 flux_ref[at : at + OWN, lanes] = sum_x[group * OWN : (group + 1) * OWN]
                 flux_ref[at + OWN : at + 2 * OWN, lanes] = sum_y[group * OWN : (group + 1) * OWN]
-            return inner
-
-        lax.fori_loop(0, NG // chunk, points, 0)
         half_ref[part] = jnp.dot(flux_ref[...].astype(BF), back_ref[...], preferred_element_type=F32) * FACTOR
         return carry
 
     lax.fori_loop(0, PARTS, line, 0)
     for quad in range(LIVE // 4):
-        parts = regroup([half_ref[part, :, quad * 128 : (quad + 1) * 128] for part in range(PARTS)])
+        rolled = []
+        for part in range(PARTS):
+            block = half_ref[part, :, quad * 128 : (quad + 1) * 128]
+            rolled.append(pltpu.roll(block, 32 * part, 1) if part else block)
         for j in range(4):
-            block = parts[j].astype(BF)
+            block = pick(masks, [rolled[(slot - j) % 4] for slot in range(4)]).astype(BF)
             for group in range(GROUPS):
                 out_ref[group, quad * 4 + j] = block[group * 16 : (group + 1) * 16]
     out_ref[:, LIVE:] = jnp.zeros((GROUPS, SLABS - LIVE, 16, 128), BF)
@@ -204,12 +233,14 @@
     row_ref, in_ref, table_ref, re_ref, im_ref, base_re_ref, base_im_ref, new_re_ref, new_im_ref, wide_ref, left_ref, prod_ref
 ):
     wide_ref[...] = in_ref[...].astype(F32).reshape(DEVS * 16, 128)
+    shift = row_ref[1]
+    slots = [lax.rem(slot + PARTS - shift, PARTS) for slot in range(PARTS)]
     for at in range(2 * OWN):
         block = wide_ref[pl.ds(at, DEVS, stride=16), :].T.astype(BF)
-        for part in range(PARTS):
+        for slot in range(PARTS):
             for c in range(2):
-                row = (part * 2 + c) * ROWS
-                left_ref[part, at * ROWS : (at + 1) * ROWS, c * QUART : (c + 1) * QUART] = block[row : row + ROWS]
+                row = (slot * 2 + c) * ROWS
+                left_ref[slots[slot], at * ROWS : (at + 1) * ROWS, c * QUART : (c + 1) * QUART] = block[row : row + ROWS]
     for part in range(PARTS):
         prod_ref[part] = (
             jnp.dot(left_ref[part], table_ref[part], preferred_element_type=F32) * FACTOR
@@ -240,7 +271,7 @@
             )
 
 
-def call(kernel, outs, scratch, specs, flops):
+def call(kernel, outs, scratch, specs, flops, limit=SMALL):
     return pl.pallas_call(
         kernel,
         out_shape=outs,
@@ -248,47 +279,52 @@
         out_specs=jax.tree.map(lambda _: pl.BlockSpec(memory_space=pltpu.VMEM), outs),
         scratch_shapes=scratch,
         cost_estimate=pl.CostEstimate(flops=flops, bytes_accessed=4 * 1024 * 1024, transcendentals=0),
-        compiler_params=pltpu.CompilerParams(vmem_limit_bytes=VMEM_LIMIT),
+        compiler_params=pltpu.CompilerParams(vmem_limit_bytes=limit),
     )
 
 
 def shards(omega_re, omega_im, base_re, base_im, triple):
     vmem = pl.BlockSpec(memory_space=pltpu.VMEM)
     smem = pl.BlockSpec(memory_space=pltpu.SMEM)
+    hbm = pl.BlockSpec(memory_space=pltpu.HBM)
     count = 3 * OWN
     ahead_x, back_x = x_tables()
     ahead_y, back_y = y_tables()
-    first_row = (lax.axis_index("grid") * ROWS).astype(jnp.int32)[None]
-    spread = np.zeros((MODES, 24 * GROUPS), np.float32)
-    for mode in range(MODES):
-        spread[mode, (mode // OWN) * 24 + mode % OWN] = 1.0
-    wide_triple = jnp.dot(
-        triple.reshape(MODES * MODES, MODES), spread.astype(ml_dtypes.bfloat16), preferred_element_type=BF
-    )
+    slab_at = lax.axis_index("grid").astype(jnp.int32)
+    place = jnp.stack([slab_at * ROWS, slab_at % PARTS])
     columns = call(
         columns_kernel,
-        jax.ShapeDtypeStruct((DEVS, count, 128), BF),
+        jax.ShapeDtypeStruct((DEVS, 24, 128), BF),
         [
+            pltpu.VMEM((OWN, ROWS, NG), F32),
+            pltpu.VMEM((OWN, ROWS, NG), F32),
+            pltpu.VMEM((PARTS, 2 * QUART, 2 * QUART), BF),
             pltpu.VMEM((PARTS, count * ROWS, 2 * QUART), BF),
             pltpu.VMEM((PARTS, count * ROWS, 2 * QUART), F32),
             pltpu.VMEM((DEVS * 24, 128), F32),
+            pltpu.SemaphoreType.DMA((2 * OWN + PARTS,)),
         ],
-        [smem, vmem, vmem, vmem],
+        [smem, hbm, hbm, hbm],
         1_000_000_000,
-    )(first_row, omega_re, omega_im, ahead_x)
+        LARGE,
+    )(place, omega_re, omega_im, ahead_x)
     slab = lax.all_to_all(columns, ("mode", "grid"), split_axis=0, concat_axis=0, tiled=True)
     halves = call(
         points_kernel,
         jax.ShapeDtypeStruct((GROUPS, SLABS, 16, 128), BF),
         [
+            pltpu.VMEM(ahead_y.shape, BF),
+            pltpu.VMEM((MODES * MODES, MODES), BF),
+            pltpu.VMEM(back_y.shape, BF),
             pltpu.VMEM((PARTS, 24 * GROUPS, NG), BF),
             pltpu.VMEM((24 * GROUPS, NG), F32),
             pltpu.VMEM((16 * GROUPS, NG), F32),
             pltpu.VMEM((PARTS, 16 * GROUPS, LIVE * 32), F32),
+            pltpu.SemaphoreType.DMA((3,)),
         ],
-        [vmem] * 4,
+        [vmem, hbm, hbm, hbm],
         10_000_000_000,
-    )(slab.reshape(GROUPS, SLABS // 4, 4, count, 128), ahead_y, wide_triple, back_y)
+    )(slab.reshape(GROUPS, SLABS // 4, 4, 24, 128), ahead_y, triple.reshape(MODES * MODES, MODES), back_y)
     rows = lax.all_to_all(halves.reshape(DEVS, 16, 128), ("mode", "grid"), split_axis=0, concat_axis=0, tiled=True)
     new = jax.ShapeDtypeStruct(base_re.shape, F32)
     return call(
@@ -301,7 +337,7 @@
         ],
         [smem] + [vmem] * 6,
         1_000_000_000,
-    )(first_row, rows, back_x, omega_re, omega_im, base_re, base_im)
+    )(place, rows, back_x, omega_re, omega_im, base_re, base_im)
 
 
 def solution(mesh):

time: 127 us -> 119 us (0.937)
  blocking collectives: 37.2 us -> 95.1 us
  waiting for transfers between devices: 40.9 us -> 0 us
  starting transfers between devices: 16.5 us -> 0 us
  local copies, waits for them, and re-layouts: 6.73 us -> 0.05 us
  Pallas kernels: 24.5 us -> 22.3 us
    all_to_all x0 -> x1, blocking collectives: none -> 57.9 us  [shards(): lax.all_to_all(columns, ('mode', 'grid'), split_axis=0, concat_axis=0, ti...]
    all_to_all x1 -> x0, waiting for transfers between devices: 40.9 us -> none  [shards(): lax.all_to_all(columns, ('mode', 'grid'), split_axis=0, concat_axis=0, ti...]
    all_to_all x1 -> x0, starting transfers between devices: 16.5 us -> none  [shards(): lax.all_to_all(columns, ('mode', 'grid'), split_axis=0, concat_axis=0, ti...]
    unnamed x24 -> x18, local copies, waits for them, and re-layouts: 6.73 us -> 0.05 us
    pallas_call x1, Pallas kernels: 18.5 us -> 13.1 us  [shards(): call(points_kernel, jax.ShapeDtypeStruct((GROUPS, SLABS, 16, 128), BF), [...]
    pallas_call x1, Pallas kernels: 3.26 us -> 5.97 us  [shards(): call(columns_kernel, jax.ShapeDtypeStruct((DEVS, 24, 128), BF), [pltpu.VM...]
  transfers between devices with their start and end apart: 1 -> 0, of which waited for: 1 -> 0; matrix products, arithmetic and copies ran while one was open for 0% -> 0% of each run, Pallas kernels for 0% -> 0%
where the time goes in v2:
time: 119 us
  blocking collectives  95.1 us (80%)
  Pallas kernels  22.3 us (19%)
    all_to_all x1, blocking collectives, shards(): lax.all_to_all(columns, ('mode', 'grid'), split_axis=0, concat_axis=0, ti...  57.9 us
    all_to_all x1, blocking collectives, shards(): lax.all_to_all(halves.reshape(DEVS, 16, 128), ('mode', 'grid'), split_axi...  37.2 us
    pallas_call x1, Pallas kernels, shards(): call(points_kernel, jax.ShapeDtypeStruct((GROUPS, SLABS, 16, 128), BF), [...  13.1 us
    pallas_call x1, Pallas kernels, shards(): call(columns_kernel, jax.ShapeDtypeStruct((DEVS, 24, 128), BF), [pltpu.VM...  5.97 us
    pallas_call x1, Pallas kernels, shards(): call(update_kernel, (new, new), [pltpu.VMEM((DEVS * 16, 128), F32), pltpu...  3.23 us

profile of v2, /device:TPU:1, one launch (start us, length us, event | category | flops | bytes accessed | tf_op | source)
XLA Modules:
  0.0 118.9 jit_solution(15952658626800228514)
XLA Ops:
  0.6 0.7 pad_add_fusion.row_ref
  1.3 0.0 copy-start.8
  1.3 6.0 %shard_map.104 = bf16[256,24,128]{2,1,0:T(8,128)(2,1)} custom-call(s32[2]{0:T(128)} %pad_add_fusion.row_ref, f32[7,16,1024]{2,1,0:T(8,128)} %re_ref.1, f32[7,16,1024]{2,1,0:T(8,128)} %im_ref.1, bf16[4,512,512]{2,1,0:T(8,128)(2,1)} %constant.27.clone.table_hbm), custom_call_target="tpu_custom_call" | custom-call | flops 1000000000 | bytes 4194304 | tf_op jit(solution)/shard_map/pallas_call | solution.py:295
  7.3 0.0 copy-start.6
  7.3 0.0 copy-start.7
  7.3 57.9 %all_to_all.10 = bf16[256,24,128]{2,1,0:T(8,128)(2,1)S(1)} all-to-all(bf16[256,24,128]{2,1,0:T(8,128)(2,1)} %shard_map.104), channel_id=1, replica_groups=mesh['mode'=8,'grid'=32] {'mode','grid'}, dimensions={0} | all-to-all | bytes 3145728 | tf_op jit(solution)/shard_map/all_to_all | solution.py:311
  65.2 0.0 copy-done.8
  65.2 0.0 copy-done.6
  65.2 0.0 copy-done.7
  65.2 0.0 copy-start.1
  65.2 0.0 copy-start.2
  65.3 0.0 copy-start.3
  65.3 0.0 copy-start.4
  65.3 13.1 %shard_map.105 = bf16[8,32,16,128]{3,2,1,0:T(8,128)(2,1)S(1)} custom-call(bf16[8,8,4,24,128]{4,3,2,1,0:T(8,128)(2,1)S(1)} %bitcast.5, bf16[1024,1024]{1,0:T(8,128)(2,1)S(1)} %copy-done.7, bf16[3136,56]{1,0:T(8,128)(2,1)S(1)} %bitcast.7, bf16[1024,768]{1,0:T(8,128)(2,1)S(1)} %copy-done.8), custom_call_target="tpu_custom_call" | custom-call | flops 10000000000 | bytes 4194304 | tf_op jit(solution)/shard_map/pallas_call | solution.py:312
  78.4 0.0 copy-start
  78.4 0.0 copy-start.5
  78.4 37.2 %all_to_all.11.in_ref = bf16[256,16,128]{2,1,0:T(8,128)(2,1)S(1)} all-to-all(bf16[256,16,128]{2,1,0:T(8,128)(2,1)S(1)} %bitcast.6), channel_id=1, replica_groups=mesh['mode'=8,'grid'=32] {'mode','grid'}, dimensions={0} | all-to-all | bytes 2097152 | tf_op jit(solution)/shard_map/all_to_all | solution.py:328
  115.6 0.0 copy-done.1
  115.6 0.0 copy-done.2
  115.7 0.0 copy-done.3
  115.7 0.0 copy-done.4
  115.7 0.0 copy-done
  115.7 0.0 copy-done.5
  115.7 3.2 %shard_map.106 = (f32[7,16,1024]{2,1,0:T(8,128)}, f32[7,16,1024]{2,1,0:T(8,128)}) custom-call(s32[2]{0:T(128)S(1)} %copy-done.5, bf16[256,16,128]{2,1,0:T(8,128)(2,1)S(1)} %all_to_all.11.in_ref, bf16[4,512,512]{2,1,0:T(8,128)(2,1)S(1)} %copy-done, f32[7,16,1024]{2,1,0:T(8,128)S(1)} %copy-done.1, f32[7,16,1024]{2,1,0:T(8,128)S(1)} %copy-done.2, ...), custom_call_target="tpu_custom_call" | custom-call | flops 1000000000 | bytes 4194304 | tf_op jit(solution)/shard_map/pallas_call | solution.py:330
Async XLA Ops:
  1.3 63.9 %copy-start.8 = (bf16[1024,768]{1,0:T(8,128)(2,1)S(1)}, bf16[1024,768]{1,0:T(8,128)(2,1)}, u32[]{:S(2)}) copy-start(bf16[1024,768]{1,0:T(8,128)(2,1)} %constant.29.clone.back_hbm) | copy-start | bytes 4718596
  7.3 57.9 %copy-start.6 = (bf16[56,56,56]{2,1,0:T(8,128)(2,1)S(1)}, bf16[56,56,56]{2,1,0:T(8,128)(2,1)}, u32[]{:S(2)}) copy-start(bf16[56,56,56]{2,1,0:T(8,128)(2,1)} %param.13) | copy-start | bytes 1053700
  7.3 57.9 %copy-start.7 = (bf16[1024,1024]{1,0:T(8,128)(2,1)S(1)}, bf16[1024,1024]{1,0:T(8,128)(2,1)}, u32[]{:S(2)}) copy-start(bf16[1024,1024]{1,0:T(8,128)(2,1)} %constant.28.clone.ahead_hbm) | copy-start | bytes 6291460
  65.2 50.4 %copy-start.1 = (f32[7,16,1024]{2,1,0:T(8,128)S(1)}, f32[7,16,1024]{2,1,0:T(8,128)}, u32[]{:S(2)}) copy-start(f32[7,16,1024]{2,1,0:T(8,128)} %re_ref.1) | copy-start | bytes 1376260
  65.2 50.4 %copy-start.2 = (f32[7,16,1024]{2,1,0:T(8,128)S(1)}, f32[7,16,1024]{2,1,0:T(8,128)}, u32[]{:S(2)}) copy-start(f32[7,16,1024]{2,1,0:T(8,128)} %im_ref.1) | copy-start | bytes 1376260
  65.3 50.4 %copy-start.3 = (f32[7,16,1024]{2,1,0:T(8,128)S(1)}, f32[7,16,1024]{2,1,0:T(8,128)}, u32[]{:S(2)}) copy-start(f32[7,16,1024]{2,1,0:T(8,128)} %base_re_ref.1) | copy-start | bytes 1376260
  65.3 50.4 %copy-start.4 = (f32[7,16,1024]{2,1,0:T(8,128)S(1)}, f32[7,16,1024]{2,1,0:T(8,128)}, u32[]{:S(2)}) copy-start(f32[7,16,1024]{2,1,0:T(8,128)} %base_im_ref.1) | copy-start | bytes 1376260
  78.4 37.2 %copy-start = (bf16[4,512,512]{2,1,0:T(8,128)(2,1)S(1)}, bf16[4,512,512]{2,1,0:T(8,128)(2,1)}, u32[]{:S(2)}) copy-start(bf16[4,512,512]{2,1,0:T(8,128)(2,1)} %constant.30.clone.table_ref) | copy-start | bytes 6291460
  78.4 37.2 %copy-start.5 = (s32[2]{0:T(128)S(1)}, s32[2]{0:T(128)}, u32[]{:S(2)}) copy-start(s32[2]{0:T(128)} %pad_add_fusion.row_ref) | copy-start | bytes 28

commit v3 on v2

--- a/solution.py
+++ b/solution.py
@@ -41,7 +41,7 @@
     for part in range(PARTS):
         points = PARTS * short + part
         cos, sin = circle(short[:, None] * points[None, :])
-        ahead.append(np.block([[cos, sin], [-sin, cos]]))
+        ahead.append(np.block([[cos, sin]]))
         cos, sin = circle(points[:, None] * short[None, :])
         back.append(np.block([[cos, -sin], [sin, cos]]))
     return (
@@ -94,8 +94,12 @@
     return along_y, along_x
 
 
+def slots_of(shift):
+    return [lax.rem(slot + PARTS - lax.rem(shift, PARTS), PARTS) for slot in range(PARTS)]
+
+
 def columns_kernel(
-    row_ref, re_hbm, im_hbm, table_hbm, out_ref, re_ref, im_ref, table_ref, left_ref, prod_ref, turn_ref, sems
+    re_hbm, im_hbm, table_hbm, out_hbm, re_ref, im_ref, table_ref, left_ref, prod_ref, turn_ref, send_ref, sems
 ):
     loads = []
     for mode in range(OWN):
@@ -106,7 +110,8 @@
             )
         )
     tables = [
-        pltpu.make_async_copy(table_hbm.at[part], table_ref.at[part], sems.at[2 * OWN + part]) for part in range(PARTS)
+        pltpu.make_async_copy(table_hbm.at[part], table_ref.at[part, pl.ds(0, QUART)], sems.at[2 * OWN + part])
+        for part in range(PARTS)
     ]
     for pair in loads:
         pair[0].start()
@@ -114,9 +119,11 @@
     for copy in tables:
         copy.start()
     count = 3 * OWN
+    half = DEVS // 2
     for at in range(count, 24):
-        turn_ref[pl.ds(at, DEVS, stride=24), :] = jnp.zeros((DEVS, 128), F32)
-    along_y, along_x = waves_of(row_ref[0])
+        turn_ref[pl.ds(at, half, stride=24), :] = jnp.zeros((half, 128), F32)
+    slab = lax.axis_index("grid")
+    along_y, along_x = waves_of(slab * ROWS)
     wave_sq = along_y * along_y + along_x * along_x
     inverse = jnp.where(wave_sq > 0.5, 1.0 / jnp.maximum(wave_sq, 1.0), 0.0)
     scale_y = along_y * inverse
@@ -141,25 +148,41 @@
                 left_ref[part, at : at + ROWS, QUART:] = b_im.astype(BF)
     for part in range(PARTS):
         tables[part].wait()
+        table_ref[part, QUART:, :QUART] = -table_ref[part, :QUART, QUART:]
+        table_ref[part, QUART:, QUART:] = table_ref[part, :QUART, :QUART]
         prod_ref[part] = (
             jnp.dot(left_ref[part], table_ref[part], preferred_element_type=F32) * FACTOR
         )
-    shift = row_ref[1]
-    slots = [lax.rem(slot + PARTS - shift, PARTS) for slot in range(PARTS)]
-    for at in range(count):
-        rows = slice(at * ROWS, (at + 1) * ROWS)
-        block = jnp.concatenate(
-            [prod_ref[slots[slot], rows, c * QUART : (c + 1) * QUART] for slot in range(PARTS) for c in range(2)],
-            axis=0,
-        )
-        turn_ref[pl.ds(at, DEVS, stride=24), :] = block.T
-    out_ref[...] = turn_ref[...].reshape(DEVS, 24, 128).astype(BF)
+    slots = slots_of(slab)
+    sends = []
+    for side in range(2):
+        for at in range(count):
+            rows = slice(at * ROWS, (at + 1) * ROWS)
+            block = jnp.concatenate(
+                [
+                    prod_ref[slots[slot], rows, c * QUART + side * half : c * QUART + (side + 1) * half]
+                    for slot in range(PARTS)
+                    for c in range(2)
+                ],
+                axis=0,
+            )
+            turn_ref[pl.ds(at, half, stride=24), :] = block.T
+        send_ref[side] = turn_ref[...].reshape(half, 24, 128).astype(BF)
+        sends.append(
+            pltpu.make_async_copy(
+                send_ref.at[side], out_hbm.at[pl.ds(side * half, half)], sems.at[2 * OWN + PARTS + side]
+            )
+        )
+        sends[side].start()
+    for copy in sends:
+        copy.wait()
 
 
 def points_kernel(
     in_ref, ahead_hbm, triple_hbm, back_hbm, out_ref, ahead_ref, triple_ref, back_ref, left_ref, phys_ref, flux_ref, half_ref, sems
 ):
     chunk = 512
+    tall = 24 * GROUPS
     ahead = pltpu.make_async_copy(ahead_hbm, ahead_ref, sems.at[0])
     couple = pltpu.make_async_copy(triple_hbm, triple_ref, sems.at[1])
     back = pltpu.make_async_copy(back_hbm, back_ref, sems.at[2])
@@ -180,21 +203,21 @@
                 sides.append(parts)
             for part in range(PARTS):
                 both = jnp.concatenate([sides[0][part], sides[1][part]], axis=0)
-                left_ref[part, pl.ds(pl.multiple_of(pair * 48, 48), 48), quad * 128 : (quad + 1) * 128] = both.astype(BF)
+                rows = pl.ds(pl.multiple_of(part * tall + pair * 48, 48), 48)
+                left_ref[rows, quad * 128 : (quad + 1) * 128] = both.astype(BF)
         return carry
 
     lax.fori_loop(0, GROUPS // 2, gather, 0)
-    flux_ref[...] = jnp.zeros_like(flux_ref)
     ahead.wait()
+    phys_ref[...] = jnp.dot(left_ref[...], ahead_ref[...], preferred_element_type=F32) * FACTOR
     couple.wait()
-    back.wait()
 
     def line(part, carry):
-        phys_ref[...] = jnp.dot(left_ref[part], ahead_ref[...], preferred_element_type=F32) * FACTOR
+        base = pl.multiple_of(part * tall, tall)
         for step in range(NG // chunk):
             lanes = slice(step * chunk, (step + 1) * chunk)
             right = jnp.concatenate(
-                [phys_ref[group * 24 : group * 24 + OWN, lanes] for group in range(GROUPS)], axis=0
+                [phys_ref[pl.ds(base + group * 24, 24), lanes][:OWN] for group in range(GROUPS)], axis=0
             ).astype(BF)
             sum_x = jnp.zeros((MODES, chunk), F32)
             sum_y = jnp.zeros((MODES, chunk), F32)
@@ -204,23 +227,24 @@
                     right,
                     preferred_element_type=F32,
                 )
-                vel = phys_ref[group * 24 : (group + 1) * 24, lanes]
+                vel = phys_ref[pl.ds(base + group * 24, 24), lanes]
                 for mode in range(OWN):
                     block = made[mode * MODES : (mode + 1) * MODES]
                     sum_x = sum_x + block * vel[OWN + mode : OWN + mode + 1]
                     sum_y = sum_y + block * vel[2 * OWN + mode : 2 * OWN + mode + 1]
             for group in range(GROUPS):
-                at = group * 16
-                flux_ref[at : at + OWN, lanes] = sum_x[group * OWN : (group + 1) * OWN]
-                flux_ref[at + OWN : at + 2 * OWN, lanes] = sum_y[group * OWN : (group + 1) * OWN]
-        half_ref[part] = jnp.dot(flux_ref[...].astype(BF), back_ref[...], preferred_element_type=F32) * FACTOR
+                own = slice(group * OWN, (group + 1) * OWN)
+                both = jnp.concatenate([sum_x[own], sum_y[own], jnp.zeros((2, chunk), F32)], axis=0)
+                flux_ref[pl.ds(pl.multiple_of((part * GROUPS + group) * 16, 16), 16), lanes] = both.astype(BF)
         return carry
 
     lax.fori_loop(0, PARTS, line, 0)
+    back.wait()
+    half_ref[...] = jnp.dot(flux_ref[...], back_ref[...], preferred_element_type=F32) * FACTOR
     for quad in range(LIVE // 4):
         rolled = []
         for part in range(PARTS):
-            block = half_ref[part, :, quad * 128 : (quad + 1) * 128]
+            block = half_ref[part * 128 : (part + 1) * 128, quad * 128 : (quad + 1) * 128]
             rolled.append(pltpu.roll(block, 32 * part, 1) if part else block)
         for j in range(4):
             block = pick(masks, [rolled[(slot - j) % 4] for slot in range(4)]).astype(BF)
@@ -230,11 +254,11 @@
 
 
 def update_kernel(
-    row_ref, in_ref, table_ref, re_ref, im_ref, base_re_ref, base_im_ref, new_re_ref, new_im_ref, wide_ref, left_ref, prod_ref
+    in_ref, table_ref, re_ref, im_ref, base_re_ref, base_im_ref, new_re, new_im, wide_ref, left_ref, prod_ref, new_re_ref, new_im_ref, sems
 ):
     wide_ref[...] = in_ref[...].astype(F32).reshape(DEVS * 16, 128)
-    shift = row_ref[1]
-    slots = [lax.rem(slot + PARTS - shift, PARTS) for slot in range(PARTS)]
+    slab = lax.axis_index("grid")
+    slots = slots_of(slab)
     for at in range(2 * OWN):
         block = wide_ref[pl.ds(at, DEVS, stride=16), :].T.astype(BF)
         for slot in range(PARTS):
@@ -245,10 +269,11 @@
         prod_ref[part] = (
             jnp.dot(left_ref[part], table_ref[part], preferred_element_type=F32) * FACTOR
         )
-    along_y, along_x = waves_of(row_ref[0])
+    along_y, along_x = waves_of(slab * ROWS)
     wave_sq = along_y * along_y + along_x * along_x
     keep = (jnp.abs(along_x) * 3.0 < NG) & (along_y * 3.0 < NG)
     damping = VISCOSITY / (NG * NG) * wave_sq
+    stores = []
     for mode in range(OWN):
         spectra = []
         for member in range(2):
@@ -269,14 +294,20 @@
             new_im_ref[mode, :, lanes] = base_im_ref[mode, :, lanes] + STEP_WEIGHT * (
                 -adv_im - damp * im_ref[mode, :, lanes]
             )
-
-
-def call(kernel, outs, scratch, specs, flops, limit=SMALL):
+        stores.append(pltpu.make_async_copy(new_re_ref.at[mode], new_re.at[mode], sems.at[2 * mode]))
+        stores.append(pltpu.make_async_copy(new_im_ref.at[mode], new_im.at[mode], sems.at[2 * mode + 1]))
+        stores[-2].start()
+        stores[-1].start()
+    for copy in stores:
+        copy.wait()
+
+
+def call(kernel, outs, scratch, specs, flops, limit=SMALL, space=pltpu.VMEM):
     return pl.pallas_call(
         kernel,
         out_shape=outs,
         in_specs=specs,
-        out_specs=jax.tree.map(lambda _: pl.BlockSpec(memory_space=pltpu.VMEM), outs),
+        out_specs=jax.tree.map(lambda _: pl.BlockSpec(memory_space=space), outs),
         scratch_shapes=scratch,
         cost_estimate=pl.CostEstimate(flops=flops, bytes_accessed=4 * 1024 * 1024, transcendentals=0),
         compiler_params=pltpu.CompilerParams(vmem_limit_bytes=limit),
@@ -285,13 +316,10 @@
 
 def shards(omega_re, omega_im, base_re, base_im, triple):
     vmem = pl.BlockSpec(memory_space=pltpu.VMEM)
-    smem = pl.BlockSpec(memory_space=pltpu.SMEM)
     hbm = pl.BlockSpec(memory_space=pltpu.HBM)
     count = 3 * OWN
     ahead_x, back_x = x_tables()
     ahead_y, back_y = y_tables()
-    slab_at = lax.axis_index("grid").astype(jnp.int32)
-    place = jnp.stack([slab_at * ROWS, slab_at % PARTS])
     columns = call(
         columns_kernel,
         jax.ShapeDtypeStruct((DEVS, 24, 128), BF),
@@ -301,13 +329,15 @@
             pltpu.VMEM((PARTS, 2 * QUART, 2 * QUART), BF),
             pltpu.VMEM((PARTS, count * ROWS, 2 * QUART), BF),
             pltpu.VMEM((PARTS, count * ROWS, 2 * QUART), F32),
-            pltpu.VMEM((DEVS * 24, 128), F32),
-            pltpu.SemaphoreType.DMA((2 * OWN + PARTS,)),
+            pltpu.VMEM((DEVS // 2 * 24, 128), F32),
+            pltpu.VMEM((2, DEVS // 2, 24, 128), BF),
+            pltpu.SemaphoreType.DMA((2 * OWN + PARTS + 2,)),
         ],
-        [smem, hbm, hbm, hbm],
+        [hbm, hbm, hbm],
         1_000_000_000,
         LARGE,
-    )(place, omega_re, omega_im, ahead_x)
+        pltpu.HBM,
+    )(omega_re, omega_im, ahead_x)
     slab = lax.all_to_all(columns, ("mode", "grid"), split_axis=0, concat_axis=0, tiled=True)
     halves = call(
         points_kernel,
@@ -316,10 +346,10 @@
             pltpu.VMEM(ahead_y.shape, BF),
             pltpu.VMEM((MODES * MODES, MODES), BF),
             pltpu.VMEM(back_y.shape, BF),
-            pltpu.VMEM((PARTS, 24 * GROUPS, NG), BF),
-            pltpu.VMEM((24 * GROUPS, NG), F32),
-            pltpu.VMEM((16 * GROUPS, NG), F32),
-            pltpu.VMEM((PARTS, 16 * GROUPS, LIVE * 32), F32),
+            pltpu.VMEM((PARTS * 24 * GROUPS, NG), BF),
+            pltpu.VMEM((PARTS * 24 * GROUPS, NG), F32),
+            pltpu.VMEM((PARTS * 16 * GROUPS, NG), BF),
+            pltpu.VMEM((PARTS * 16 * GROUPS, LIVE * 32), F32),
             pltpu.SemaphoreType.DMA((3,)),
         ],
         [vmem, hbm, hbm, hbm],
@@ -334,10 +364,15 @@
             pltpu.VMEM((DEVS * 16, 128), F32),
             pltpu.VMEM((PARTS, 2 * OWN * ROWS, 2 * QUART), BF),
             pltpu.VMEM((PARTS, 2 * OWN * ROWS, 2 * QUART), F32),
+            pltpu.VMEM(base_re.shape, F32),
+            pltpu.VMEM(base_re.shape, F32),
+            pltpu.SemaphoreType.DMA((2 * OWN,)),
         ],
-        [smem] + [vmem] * 6,
+        [vmem] * 6,
         1_000_000_000,
-    )(place, rows, back_x, omega_re, omega_im, base_re, base_im)
+        SMALL,
+        pltpu.HBM,
+    )(rows, back_x, omega_re, omega_im, base_re, base_im)
 
 
 def solution(mesh):

time: 119 us -> 116 us (0.975)
  Pallas kernels: 22.3 us -> 20 us
where the time goes in v3:
time: 116 us
  blocking collectives  95.1 us (82%)
  Pallas kernels  20 us (17%)
    all_to_all x1, blocking collectives, shards(): lax.all_to_all(columns, ('mode', 'grid'), split_axis=0, concat_axis=0, ti...  57.9 us
    all_to_all x1, blocking collectives, shards(): lax.all_to_all(halves.reshape(DEVS, 16, 128), ('mode', 'grid'), split_axi...  37.2 us
    pallas_call x1, Pallas kernels, shards(): call(points_kernel, jax.ShapeDtypeStruct((GROUPS, SLABS, 16, 128), BF), [...  12.6 us
    pallas_call x1, Pallas kernels, shards(): call(columns_kernel, jax.ShapeDtypeStruct((DEVS, 24, 128), BF), [pltpu.VM...  4.85 us
    pallas_call x1, Pallas kernels, shards(): call(update_kernel, (new, new), [pltpu.VMEM((DEVS * 16, 128), F32), pltpu...  2.51 us

profile of v3, /device:TPU:1, one launch (start us, length us, event | category | flops | bytes accessed | tf_op | source)
XLA Modules:
  0.0 115.9 jit_solution(15249657795941729291)
XLA Ops:
  0.6 0.0 copy-start.7
  0.6 4.8 %shard_map.104 = bf16[256,24,128]{2,1,0:T(8,128)(2,1)} custom-call(f32[7,16,1024]{2,1,0:T(8,128)} %re_ref.1, f32[7,16,1024]{2,1,0:T(8,128)} %im_ref.1, bf16[4,256,512]{2,1,0:T(8,128)(2,1)} %constant.8.clone.table_hbm), custom_call_target="tpu_custom_call" | custom-call | flops 1000000000 | bytes 4194304 | tf_op jit(solution)/shard_map/pallas_call | solution.py:323
  5.5 0.0 copy-start.5
  5.5 0.0 copy-start.6
  5.5 57.9 %all_to_all.10 = bf16[256,24,128]{2,1,0:T(8,128)(2,1)S(1)} all-to-all(bf16[256,24,128]{2,1,0:T(8,128)(2,1)} %shard_map.104), channel_id=1, replica_groups=mesh['mode'=8,'grid'=32] {'mode','grid'}, dimensions={0} | all-to-all | bytes 3145728 | tf_op jit(solution)/shard_map/all_to_all | solution.py:341
  63.4 0.0 copy-done.7
  63.4 0.0 copy-done.5
  63.4 0.0 copy-done.6
  63.4 0.0 copy-start.1
  63.5 0.0 copy-start.2
  63.5 0.0 copy-start.3
  63.5 0.0 copy-start.4
  63.5 12.6 %shard_map.105 = bf16[8,32,16,128]{3,2,1,0:T(8,128)(2,1)S(1)} custom-call(bf16[8,8,4,24,128]{4,3,2,1,0:T(8,128)(2,1)S(1)} %bitcast.3, bf16[1024,1024]{1,0:T(8,128)(2,1)S(1)} %copy-done.6, bf16[3136,56]{1,0:T(8,128)(2,1)S(1)} %bitcast.5, bf16[1024,768]{1,0:T(8,128)(2,1)S(1)} %copy-done.7), custom_call_target="tpu_custom_call" | custom-call | flops 10000000000 | bytes 4194304 | tf_op jit(solution)/shard_map/pallas_call | solution.py:342
  76.1 0.0 copy-start
  76.1 37.2 %all_to_all.11.in_ref = bf16[256,16,128]{2,1,0:T(8,128)(2,1)S(1)} all-to-all(bf16[256,16,128]{2,1,0:T(8,128)(2,1)S(1)} %bitcast.4), channel_id=1, replica_groups=mesh['mode'=8,'grid'=32] {'mode','grid'}, dimensions={0} | all-to-all | bytes 2097152 | tf_op jit(solution)/shard_map/all_to_all | solution.py:358
  113.3 0.0 copy-done.1
  113.3 0.0 copy-done.2
  113.3 0.0 copy-done.3
  113.4 0.0 copy-done.4
  113.4 0.0 copy-done
  113.4 2.5 %shard_map.106 = (f32[7,16,1024]{2,1,0:T(8,128)}, f32[7,16,1024]{2,1,0:T(8,128)}) custom-call(bf16[256,16,128]{2,1,0:T(8,128)(2,1)S(1)} %all_to_all.11.in_ref, bf16[4,512,512]{2,1,0:T(8,128)(2,1)S(1)} %copy-done, f32[7,16,1024]{2,1,0:T(8,128)S(1)} %copy-done.1, f32[7,16,1024]{2,1,0:T(8,128)S(1)} %copy-done.2, f32[7,16,1024]{2,1,0:T(8,128)S(1)} %copy-done.3, ...), custom_call_target="tpu_custom_call" | custom-call | flops 1000000000 | bytes 4194304 | tf_op jit(solution)/shard_map/pallas_call | solution.py:360
Async XLA Ops:
  0.6 62.8 %copy-start.7 = (bf16[1024,768]{1,0:T(8,128)(2,1)S(1)}, bf16[1024,768]{1,0:T(8,128)(2,1)}, u32[]{:S(2)}) copy-start(bf16[1024,768]{1,0:T(8,128)(2,1)} %constant.10.clone.back_hbm) | copy-start | bytes 4718596
  5.5 57.9 %copy-start.5 = (bf16[56,56,56]{2,1,0:T(8,128)(2,1)S(1)}, bf16[56,56,56]{2,1,0:T(8,128)(2,1)}, u32[]{:S(2)}) copy-start(bf16[56,56,56]{2,1,0:T(8,128)(2,1)} %param.13) | copy-start | bytes 1053700
  5.5 57.9 %copy-start.6 = (bf16[1024,1024]{1,0:T(8,128)(2,1)S(1)}, bf16[1024,1024]{1,0:T(8,128)(2,1)}, u32[]{:S(2)}) copy-start(bf16[1024,1024]{1,0:T(8,128)(2,1)} %constant.9.clone.ahead_hbm) | copy-start | bytes 6291460
  63.4 49.9 %copy-start.1 = (f32[7,16,1024]{2,1,0:T(8,128)S(1)}, f32[7,16,1024]{2,1,0:T(8,128)}, u32[]{:S(2)}) copy-start(f32[7,16,1024]{2,1,0:T(8,128)} %re_ref.1) | copy-start | bytes 1376260
  63.5 49.9 %copy-start.2 = (f32[7,16,1024]{2,1,0:T(8,128)S(1)}, f32[7,16,1024]{2,1,0:T(8,128)}, u32[]{:S(2)}) copy-start(f32[7,16,1024]{2,1,0:T(8,128)} %im_ref.1) | copy-start | bytes 1376260
  63.5 49.9 %copy-start.3 = (f32[7,16,1024]{2,1,0:T(8,128)S(1)}, f32[7,16,1024]{2,1,0:T(8,128)}, u32[]{:S(2)}) copy-start(f32[7,16,1024]{2,1,0:T(8,128)} %base_re_ref.1) | copy-start | bytes 1376260
  63.5 49.9 %copy-start.4 = (f32[7,16,1024]{2,1,0:T(8,128)S(1)}, f32[7,16,1024]{2,1,0:T(8,128)}, u32[]{:S(2)}) copy-start(f32[7,16,1024]{2,1,0:T(8,128)} %base_im_ref.1) | copy-start | bytes 1376260
  76.1 37.2 %copy-start = (bf16[4,512,512]{2,1,0:T(8,128)(2,1)S(1)}, bf16[4,512,512]{2,1,0:T(8,128)(2,1)}, u32[]{:S(2)}) copy-start(bf16[4,512,512]{2,1,0:T(8,128)(2,1)} %constant.11.clone.table_ref) | copy-start | bytes 6291460

commit v4 on v3

--- a/solution.py
+++ b/solution.py
@@ -23,6 +23,8 @@
 PARTS = NG // DEVS
 QUART = NG // 4
 FACTOR = 1.0 / math.sqrt(NG)
+OUT = 22
+HOME = 2 * OWN
 LIVE = 24
 BF = jnp.bfloat16
 F32 = jnp.float32
@@ -120,8 +122,8 @@
         copy.start()
     count = 3 * OWN
     half = DEVS // 2
-    for at in range(count, 24):
-        turn_ref[pl.ds(at, half, stride=24), :] = jnp.zeros((half, 128), F32)
+    for at in range(count, OUT):
+        turn_ref[pl.ds(at, half, stride=OUT), :] = jnp.zeros((half, 128), F32)
     slab = lax.axis_index("grid")
     along_y, along_x = waves_of(slab * ROWS)
     wave_sq = along_y * along_y + along_x * along_x
@@ -166,11 +168,11 @@
                 ],
                 axis=0,
             )
-            turn_ref[pl.ds(at, half, stride=24), :] = block.T
-        send_ref[side] = turn_ref[...].reshape(half, 24, 128).astype(BF)
+            turn_ref[pl.ds(at, half, stride=OUT), :] = block.T
+        send_ref[side] = turn_ref[...].astype(BF)
         sends.append(
             pltpu.make_async_copy(
-                send_ref.at[side], out_hbm.at[pl.ds(side * half, half)], sems.at[2 * OWN + PARTS + side]
+                send_ref.at[side], out_hbm.at[pl.ds(side * half * OUT, half * OUT)], sems.at[2 * OWN + PARTS + side]
             )
         )
         sends[side].start()
@@ -179,7 +181,7 @@
 
 
 def points_kernel(
-    in_ref, ahead_hbm, triple_hbm, back_hbm, out_ref, ahead_ref, triple_ref, back_ref, left_ref, phys_ref, flux_ref, half_ref, sems
+    in_ref, ahead_hbm, triple_hbm, back_hbm, out_ref, ahead_ref, triple_ref, back_ref, wide_ref, left_ref, phys_ref, flux_ref, half_ref, send_ref, sems
 ):
     chunk = 512
     tall = 24 * GROUPS
@@ -190,12 +192,17 @@
     couple.start()
     back.start()
     masks = lane_masks()
+    span = SLABS * OUT
+    for side in range(2):
+        wide_ref[side, span:] = jnp.zeros((8, 128), F32)
 
     def gather(pair, carry):
+        for side in range(2):
+            wide_ref[side, :span] = in_ref[pl.ds(pl.multiple_of((pair * 2 + side) * span, span), span)].astype(F32)
         for quad in range(SLABS // 4):
             sides = []
             for side in range(2):
-                blocks = [in_ref[pair * 2 + side, quad, j].astype(F32) for j in range(4)]
+                blocks = [wide_ref[side, (quad * 4 + j) * OUT : (quad * 4 + j) * OUT + 24] for j in range(4)]
                 parts = []
                 for part in range(PARTS):
                     mixed = pick(masks, [blocks[(slot - part) % 4] for slot in range(4)])
@@ -247,20 +254,24 @@
             block = half_ref[part * 128 : (part + 1) * 128, quad * 128 : (quad + 1) * 128]
             rolled.append(pltpu.roll(block, 32 * part, 1) if part else block)
         for j in range(4):
-            block = pick(masks, [rolled[(slot - j) % 4] for slot in range(4)]).astype(BF)
+            block = pick(masks, [rolled[(slot - j) % 4] for slot in range(4)])
             for group in range(GROUPS):
-                out_ref[group, quad * 4 + j] = block[group * 16 : (group + 1) * 16]
-    out_ref[:, LIVE:] = jnp.zeros((GROUPS, SLABS - LIVE, 16, 128), BF)
+                at = (group * SLABS + quad * 4 + j) * HOME
+                send_ref[at : at + HOME] = block[group * 16 : group * 16 + HOME]
+    for group in range(GROUPS):
+        at = (group * SLABS + LIVE) * HOME
+        send_ref[at : at + (SLABS - LIVE) * HOME] = jnp.zeros(((SLABS - LIVE) * HOME, 128), F32)
+    out_ref[...] = send_ref[...].astype(BF)
 
 
 def update_kernel(
     in_ref, table_ref, re_ref, im_ref, base_re_ref, base_im_ref, new_re, new_im, wide_ref, left_ref, prod_ref, new_re_ref, new_im_ref, sems
 ):
-    wide_ref[...] = in_ref[...].astype(F32).reshape(DEVS * 16, 128)
+    wide_ref[...] = in_ref[...].astype(F32)
     slab = lax.axis_index("grid")
     slots = slots_of(slab)
     for at in range(2 * OWN):
-        block = wide_ref[pl.ds(at, DEVS, stride=16), :].T.astype(BF)
+        block = wide_ref[pl.ds(at, DEVS, stride=HOME), :].T.astype(BF)
         for slot in range(PARTS):
             for c in range(2):
                 row = (slot * 2 + c) * ROWS
@@ -314,6 +325,12 @@
     )
 
 
+def exchange(array, count):
+    blocks = array.reshape(DEVS, count // 2, 2, 128)
+    blocks = lax.all_to_all(blocks, ("mode", "grid"), split_axis=0, concat_axis=0, tiled=True)
+    return blocks.reshape(DEVS * count, 128)
+
+
 def shards(omega_re, omega_im, base_re, base_im, triple):
     vmem = pl.BlockSpec(memory_space=pltpu.VMEM)
     hbm = pl.BlockSpec(memory_space=pltpu.HBM)
@@ -322,15 +339,15 @@
     ahead_y, back_y = y_tables()
     columns = call(
         columns_kernel,
-        jax.ShapeDtypeStruct((DEVS, 24, 128), BF),
+        jax.ShapeDtypeStruct((DEVS * OUT, 128), BF),
         [
             pltpu.VMEM((OWN, ROWS, NG), F32),
             pltpu.VMEM((OWN, ROWS, NG), F32),
             pltpu.VMEM((PARTS, 2 * QUART, 2 * QUART), BF),
             pltpu.VMEM((PARTS, count * ROWS, 2 * QUART), BF),
             pltpu.VMEM((PARTS, count * ROWS, 2 * QUART), F32),
-            pltpu.VMEM((DEVS // 2 * 24, 128), F32),
-            pltpu.VMEM((2, DEVS // 2, 24, 128), BF),
+            pltpu.VMEM((DEVS // 2 * OUT, 128), F32),
+            pltpu.VMEM((2, DEVS // 2 * OUT, 128), BF),
             pltpu.SemaphoreType.DMA((2 * OWN + PARTS + 2,)),
         ],
         [hbm, hbm, hbm],
@@ -338,30 +355,32 @@
         LARGE,
         pltpu.HBM,
     )(omega_re, omega_im, ahead_x)
-    slab = lax.all_to_all(columns, ("mode", "grid"), split_axis=0, concat_axis=0, tiled=True)
+    slab = exchange(columns, OUT)
     halves = call(
         points_kernel,
-        jax.ShapeDtypeStruct((GROUPS, SLABS, 16, 128), BF),
+        jax.ShapeDtypeStruct((DEVS * HOME, 128), BF),
         [
             pltpu.VMEM(ahead_y.shape, BF),
             pltpu.VMEM((MODES * MODES, MODES), BF),
             pltpu.VMEM(back_y.shape, BF),
+            pltpu.VMEM((2, SLABS * OUT + 8, 128), F32),
             pltpu.VMEM((PARTS * 24 * GROUPS, NG), BF),
             pltpu.VMEM((PARTS * 24 * GROUPS, NG), F32),
             pltpu.VMEM((PARTS * 16 * GROUPS, NG), BF),
             pltpu.VMEM((PARTS * 16 * GROUPS, LIVE * 32), F32),
+            pltpu.VMEM((DEVS * HOME, 128), F32),
             pltpu.SemaphoreType.DMA((3,)),
         ],
         [vmem, hbm, hbm, hbm],
         10_000_000_000,
-    )(slab.reshape(GROUPS, SLABS // 4, 4, 24, 128), ahead_y, triple.reshape(MODES * MODES, MODES), back_y)
-    rows = lax.all_to_all(halves.reshape(DEVS, 16, 128), ("mode", "grid"), split_axis=0, concat_axis=0, tiled=True)
+    )(slab, ahead_y, triple.reshape(MODES * MODES, MODES), back_y)
+    rows = exchange(halves, HOME)
     new = jax.ShapeDtypeStruct(base_re.shape, F32)
     return call(
         update_kernel,
         (new, new),
         [
-            pltpu.VMEM((DEVS * 16, 128), F32),
+            pltpu.VMEM((DEVS * HOME, 128), F32),
             pltpu.VMEM((PARTS, 2 * OWN * ROWS, 2 * QUART), BF),
             pltpu.VMEM((PARTS, 2 * OWN * ROWS, 2 * QUART), F32),
             pltpu.VMEM(base_re.shape, F32),

time: 116 us -> 111 us (0.957)
  blocking collectives: 95.1 us -> 89.5 us
    all_to_all x2, blocking collectives: 95.1 us -> 89.5 us  [exchange(): lax.all_to_all(blocks, ('mode', 'grid'), split_axis=0, concat_axis=0, til...]
where the time goes in v4:
time: 111 us
  blocking collectives  89.5 us (81%)
  Pallas kernels  20.5 us (18%)
    all_to_all x2, blocking collectives, exchange(): lax.all_to_all(blocks, ('mode', 'grid'), split_axis=0, concat_axis=0, til...  89.5 us
    pallas_call x1, Pallas kernels, shards(): call(points_kernel, jax.ShapeDtypeStruct((DEVS * HOME, 128), BF), [pltpu....  13.4 us
    pallas_call x1, Pallas kernels, shards(): call(columns_kernel, jax.ShapeDtypeStruct((DEVS * OUT, 128), BF), [pltpu....  4.85 us
    pallas_call x1, Pallas kernels, shards(): call(update_kernel, (new, new), [pltpu.VMEM((DEVS * HOME, 128), F32), plt...  2.26 us

profile of v4, /device:TPU:1, one launch (start us, length us, event | category | flops | bytes accessed | tf_op | source)
XLA Modules:
  0.0 110.8 jit_solution(14760725807018156847)
XLA Ops:
  0.6 0.0 copy-start.6
  0.6 4.9 %shard_map.104 = bf16[5632,128]{1,0:T(8,128)(2,1)} custom-call(f32[7,16,1024]{2,1,0:T(8,128)} %re_ref.1, f32[7,16,1024]{2,1,0:T(8,128)} %im_ref.1, bf16[4,256,512]{2,1,0:T(8,128)(2,1)} %constant.8.clone.table_hbm), custom_call_target="tpu_custom_call" | custom-call | flops 1000000000 | bytes 4194304 | tf_op jit(solution)/shard_map/pallas_call | solution.py:340
  5.5 0.0 copy-start.5
  5.5 0.0 copy-start.7
  5.5 55.1 %all_to_all.10 = bf16[256,11,2,128]{3,2,1,0:T(2,128)(2,1)S(1)} all-to-all(bf16[256,11,2,128]{3,2,1,0:T(2,128)(2,1)} %bitcast.9), channel_id=1, replica_groups=mesh['mode'=8,'grid'=32] {'mode','grid'}, dimensions={0} | all-to-all | bytes 2883584 | tf_op jit(solution)/shard_map/all_to_all | solution.py:330
  60.6 0.0 copy-done.6
  60.6 0.0 copy-done.5
  60.7 0.0 copy-done.7
  60.7 0.0 copy-start
  60.7 13.4 %shard_map.105 = bf16[3584,128]{1,0:T(8,128)(2,1)S(1)} custom-call(bf16[5632,128]{1,0:T(8,128)(2,1)S(1)} %bitcast.6, bf16[1024,1024]{1,0:T(8,128)(2,1)S(1)} %copy-done.6, bf16[3136,56]{1,0:T(8,128)(2,1)S(1)} %bitcast.8, bf16[1024,768]{1,0:T(8,128)(2,1)S(1)} %copy-done.7), custom_call_target="tpu_custom_call" | custom-call | flops 10000000000 | bytes 4194304 | tf_op jit(solution)/shard_map/pallas_call | solution.py:359
  74.0 0.0 copy-start.1
  74.1 0.0 copy-start.2
  74.1 0.0 copy-start.3
  74.1 0.0 copy-start.4
  74.1 34.4 %all_to_all.11 = bf16[256,7,2,128]{3,2,1,0:T(2,128)(2,1)S(1)} all-to-all(bf16[256,7,2,128]{3,2,1,0:T(2,128)(2,1)S(1)} %bitcast.7), channel_id=1, replica_groups=mesh['mode'=8,'grid'=32] {'mode','grid'}, dimensions={0} | all-to-all | bytes 1835008 | tf_op jit(solution)/shard_map/all_to_all | solution.py:330
  108.5 0.0 copy-done
  108.5 0.0 copy-done.1
  108.5 0.0 copy-done.2
  108.5 0.0 copy-done.3
  108.5 0.0 copy-done.4
  108.5 2.3 %shard_map.106 = (f32[7,16,1024]{2,1,0:T(8,128)}, f32[7,16,1024]{2,1,0:T(8,128)}) custom-call(bf16[3584,128]{1,0:T(8,128)(2,1)S(1)} %bitcast.5, bf16[4,512,512]{2,1,0:T(8,128)(2,1)S(1)} %copy-done, f32[7,16,1024]{2,1,0:T(8,128)S(1)} %copy-done.1, f32[7,16,1024]{2,1,0:T(8,128)S(1)} %copy-done.2, f32[7,16,1024]{2,1,0:T(8,128)S(1)} %copy-done.3, ...), custom_call_target="tpu_custom_call" | custom-call | flops 1000000000 | bytes 4194304 | tf_op jit(solution)/shard_map/pallas_call | solution.py:379
Async XLA Ops:
  0.6 60.0 %copy-start.6 = (bf16[1024,1024]{1,0:T(8,128)(2,1)S(1)}, bf16[1024,1024]{1,0:T(8,128)(2,1)}, u32[]{:S(2)}) copy-start(bf16[1024,1024]{1,0:T(8,128)(2,1)} %constant.9.clone.ahead_hbm) | copy-start | bytes 6291460
  5.5 55.1 %copy-start.5 = (bf16[56,56,56]{2,1,0:T(8,128)(2,1)S(1)}, bf16[56,56,56]{2,1,0:T(8,128)(2,1)}, u32[]{:S(2)}) copy-start(bf16[56,56,56]{2,1,0:T(8,128)(2,1)} %param.13) | copy-start | bytes 1053700
  5.5 55.1 %copy-start.7 = (bf16[1024,768]{1,0:T(8,128)(2,1)S(1)}, bf16[1024,768]{1,0:T(8,128)(2,1)}, u32[]{:S(2)}) copy-start(bf16[1024,768]{1,0:T(8,128)(2,1)} %constant.10.clone.back_hbm) | copy-start | bytes 4718596
  60.7 47.8 %copy-start = (bf16[4,512,512]{2,1,0:T(8,128)(2,1)S(1)}, bf16[4,512,512]{2,1,0:T(8,128)(2,1)}, u32[]{:S(2)}) copy-start(bf16[4,512,512]{2,1,0:T(8,128)(2,1)} %constant.11.clone.table_ref) | copy-start | bytes 6291460
  74.0 34.4 %copy-start.1 = (f32[7,16,1024]{2,1,0:T(8,128)S(1)}, f32[7,16,1024]{2,1,0:T(8,128)}, u32[]{:S(2)}) copy-start(f32[7,16,1024]{2,1,0:T(8,128)} %re_ref.1) | copy-start | bytes 1376260
  74.1 34.4 %copy-start.2 = (f32[7,16,1024]{2,1,0:T(8,128)S(1)}, f32[7,16,1024]{2,1,0:T(8,128)}, u32[]{:S(2)}) copy-start(f32[7,16,1024]{2,1,0:T(8,128)} %im_ref.1) | copy-start | bytes 1376260
  74.1 34.4 %copy-start.3 = (f32[7,16,1024]{2,1,0:T(8,128)S(1)}, f32[7,16,1024]{2,1,0:T(8,128)}, u32[]{:S(2)}) copy-start(f32[7,16,1024]{2,1,0:T(8,128)} %base_re_ref.1) | copy-start | bytes 1376260
  74.1 34.4 %copy-start.4 = (f32[7,16,1024]{2,1,0:T(8,128)S(1)}, f32[7,16,1024]{2,1,0:T(8,128)}, u32[]{:S(2)}) copy-start(f32[7,16,1024]{2,1,0:T(8,128)} %base_im_ref.1) | copy-start | bytes 1376260

commit v5 on v4

--- a/solution.py
+++ b/solution.py
@@ -181,16 +181,10 @@
 
 
 def points_kernel(
-    in_ref, ahead_hbm, triple_hbm, back_hbm, out_ref, ahead_ref, triple_ref, back_ref, wide_ref, left_ref, phys_ref, flux_ref, half_ref, send_ref, sems
+    in_ref, ahead_ref, triple_ref, back_ref, out_ref, wide_ref, left_ref, phys_ref, flux_ref, half_ref, send_ref
 ):
     chunk = 512
     tall = 24 * GROUPS
-    ahead = pltpu.make_async_copy(ahead_hbm, ahead_ref, sems.at[0])
-    couple = pltpu.make_async_copy(triple_hbm, triple_ref, sems.at[1])
-    back = pltpu.make_async_copy(back_hbm, back_ref, sems.at[2])
-    ahead.start()
-    couple.start()
-    back.start()
     masks = lane_masks()
     span = SLABS * OUT
     for side in range(2):
@@ -214,10 +208,8 @@
                 left_ref[rows, quad * 128 : (quad + 1) * 128] = both.astype(BF)
         return carry
 
-    lax.fori_loop(0, GROUPS // 2, gather, 0)
-    ahead.wait()
+    lax.fori_loop(0, GROUPS // 2, gather, 0, unroll=True)
     phys_ref[...] = jnp.dot(left_ref[...], ahead_ref[...], preferred_element_type=F32) * FACTOR
-    couple.wait()
 
     def line(part, carry):
         base = pl.multiple_of(part * tall, tall)
@@ -246,7 +238,6 @@
         return carry
 
     lax.fori_loop(0, PARTS, line, 0)
-    back.wait()
     half_ref[...] = jnp.dot(flux_ref[...], back_ref[...], preferred_element_type=F32) * FACTOR
     for quad in range(LIVE // 4):
         rolled = []
@@ -360,18 +351,14 @@
         points_kernel,
         jax.ShapeDtypeStruct((DEVS * HOME, 128), BF),
         [
-            pltpu.VMEM(ahead_y.shape, BF),
-            pltpu.VMEM((MODES * MODES, MODES), BF),
-            pltpu.VMEM(back_y.shape, BF),
             pltpu.VMEM((2, SLABS * OUT + 8, 128), F32),
             pltpu.VMEM((PARTS * 24 * GROUPS, NG), BF),
             pltpu.VMEM((PARTS * 24 * GROUPS, NG), F32),
             pltpu.VMEM((PARTS * 16 * GROUPS, NG), BF),
             pltpu.VMEM((PARTS * 16 * GROUPS, LIVE * 32), F32),
             pltpu.VMEM((DEVS * HOME, 128), F32),
-            pltpu.SemaphoreType.DMA((3,)),
         ],
-        [vmem, hbm, hbm, hbm],
+        [vmem] * 4,
         10_000_000_000,
     )(slab, ahead_y, triple.reshape(MODES * MODES, MODES), back_y)
     rows = exchange(halves, HOME)

time: 111 us -> 110 us (level)
  no operation moved by 1% of the time
where the time goes in v5:
time: 110 us
  blocking collectives  89.5 us (81%)
  Pallas kernels  19.5 us (18%)
    all_to_all x2, blocking collectives, exchange(): lax.all_to_all(blocks, ('mode', 'grid'), split_axis=0, concat_axis=0, til...  89.5 us
    pallas_call x1, Pallas kernels, shards(): call(points_kernel, jax.ShapeDtypeStruct((DEVS * HOME, 128), BF), [pltpu....  12.4 us
    pallas_call x1, Pallas kernels, shards(): call(columns_kernel, jax.ShapeDtypeStruct((DEVS * OUT, 128), BF), [pltpu....  4.85 us
    pallas_call x1, Pallas kernels, shards(): call(update_kernel, (new, new), [pltpu.VMEM((DEVS * HOME, 128), F32), plt...  2.26 us

profile of v5, /device:TPU:1, one launch (start us, length us, event | category | flops | bytes accessed | tf_op | source)
XLA Modules:
  0.0 109.8 jit_solution(9287978473452627233)
XLA Ops:
  0.6 0.0 copy-start.6
  0.6 4.9 %shard_map.104 = bf16[5632,128]{1,0:T(8,128)(2,1)} custom-call(f32[7,16,1024]{2,1,0:T(8,128)} %re_ref.1, f32[7,16,1024]{2,1,0:T(8,128)} %im_ref.1, bf16[4,256,512]{2,1,0:T(8,128)(2,1)} %constant.8.clone.table_hbm), custom_call_target="tpu_custom_call" | custom-call | flops 1000000000 | bytes 4194304 | tf_op jit(solution)/shard_map/pallas_call | solution.py:331
  5.5 0.0 copy-start.5
  5.5 0.0 copy-start.7
  5.5 55.1 %all_to_all.10 = bf16[256,11,2,128]{3,2,1,0:T(2,128)(2,1)S(1)} all-to-all(bf16[256,11,2,128]{3,2,1,0:T(2,128)(2,1)} %bitcast.9), channel_id=1, replica_groups=mesh['mode'=8,'grid'=32] {'mode','grid'}, dimensions={0} | all-to-all | bytes 2883584 | tf_op jit(solution)/shard_map/all_to_all | solution.py:321
  60.6 0.0 copy-done.6
  60.6 0.0 copy-done.5
  60.7 0.0 copy-done.7
  60.7 0.0 copy-start
  60.7 12.4 %shard_map.105 = bf16[3584,128]{1,0:T(8,128)(2,1)S(1)} custom-call(bf16[5632,128]{1,0:T(8,128)(2,1)S(1)} %bitcast.6, bf16[1024,1024]{1,0:T(8,128)(2,1)S(1)} %copy-done.6, bf16[3136,56]{1,0:T(8,128)(2,1)S(1)} %bitcast.8, bf16[1024,768]{1,0:T(8,128)(2,1)S(1)} %copy-done.7), custom_call_target="tpu_custom_call" | custom-call | flops 10000000000 | bytes 4194304 | tf_op jit(solution)/shard_map/pallas_call | solution.py:350
  73.1 0.0 copy-start.1
  73.1 0.0 copy-start.2
  73.1 0.0 copy-start.3
  73.1 0.0 copy-start.4
  73.1 34.4 %all_to_all.11 = bf16[256,7,2,128]{3,2,1,0:T(2,128)(2,1)S(1)} all-to-all(bf16[256,7,2,128]{3,2,1,0:T(2,128)(2,1)S(1)} %bitcast.7), channel_id=1, replica_groups=mesh['mode'=8,'grid'=32] {'mode','grid'}, dimensions={0} | all-to-all | bytes 1835008 | tf_op jit(solution)/shard_map/all_to_all | solution.py:321
  107.5 0.0 copy-done
  107.5 0.0 copy-done.1
  107.5 0.0 copy-done.2
  107.5 0.0 copy-done.3
  107.5 0.0 copy-done.4
  107.5 2.3 %shard_map.106 = (f32[7,16,1024]{2,1,0:T(8,128)}, f32[7,16,1024]{2,1,0:T(8,128)}) custom-call(bf16[3584,128]{1,0:T(8,128)(2,1)S(1)} %bitcast.5, bf16[4,512,512]{2,1,0:T(8,128)(2,1)S(1)} %copy-done, f32[7,16,1024]{2,1,0:T(8,128)S(1)} %copy-done.1, f32[7,16,1024]{2,1,0:T(8,128)S(1)} %copy-done.2, f32[7,16,1024]{2,1,0:T(8,128)S(1)} %copy-done.3, ...), custom_call_target="tpu_custom_call" | custom-call | flops 1000000000 | bytes 4194304 | tf_op jit(solution)/shard_map/pallas_call | solution.py:366
Async XLA Ops:
  0.6 60.0 %copy-start.6 = (bf16[1024,1024]{1,0:T(8,128)(2,1)S(1)}, bf16[1024,1024]{1,0:T(8,128)(2,1)}, u32[]{:S(2)}) copy-start(bf16[1024,1024]{1,0:T(8,128)(2,1)} %constant.9.clone.ahead_ref) | copy-start | bytes 6291460
  5.5 55.1 %copy-start.5 = (bf16[56,56,56]{2,1,0:T(8,128)(2,1)S(1)}, bf16[56,56,56]{2,1,0:T(8,128)(2,1)}, u32[]{:S(2)}) copy-start(bf16[56,56,56]{2,1,0:T(8,128)(2,1)} %param.13) | copy-start | bytes 1053700
  5.5 55.1 %copy-start.7 = (bf16[1024,768]{1,0:T(8,128)(2,1)S(1)}, bf16[1024,768]{1,0:T(8,128)(2,1)}, u32[]{:S(2)}) copy-start(bf16[1024,768]{1,0:T(8,128)(2,1)} %constant.10.clone.back_ref) | copy-start | bytes 4718596
  60.7 46.9 %copy-start = (bf16[4,512,512]{2,1,0:T(8,128)(2,1)S(1)}, bf16[4,512,512]{2,1,0:T(8,128)(2,1)}, u32[]{:S(2)}) copy-start(bf16[4,512,512]{2,1,0:T(8,128)(2,1)} %constant.11.clone.table_ref) | copy-start | bytes 6291460
  73.1 34.4 %copy-start.1 = (f32[7,16,1024]{2,1,0:T(8,128)S(1)}, f32[7,16,1024]{2,1,0:T(8,128)}, u32[]{:S(2)}) copy-start(f32[7,16,1024]{2,1,0:T(8,128)} %re_ref.1) | copy-start | bytes 1376260
  73.1 34.4 %copy-start.2 = (f32[7,16,1024]{2,1,0:T(8,128)S(1)}, f32[7,16,1024]{2,1,0:T(8,128)}, u32[]{:S(2)}) copy-start(f32[7,16,1024]{2,1,0:T(8,128)} %im_ref.1) | copy-start | bytes 1376260
  73.1 34.4 %copy-start.3 = (f32[7,16,1024]{2,1,0:T(8,128)S(1)}, f32[7,16,1024]{2,1,0:T(8,128)}, u32[]{:S(2)}) copy-start(f32[7,16,1024]{2,1,0:T(8,128)} %base_re_ref.1) | copy-start | bytes 1376260
  73.1 34.4 %copy-start.4 = (f32[7,16,1024]{2,1,0:T(8,128)S(1)}, f32[7,16,1024]{2,1,0:T(8,128)}, u32[]{:S(2)}) copy-start(f32[7,16,1024]{2,1,0:T(8,128)} %base_im_ref.1) | copy-start | bytes 1376260

commit v6 on v5

--- a/solution.py
+++ b/solution.py
@@ -20,6 +20,7 @@
 DEVS = GROUPS * SLABS
 OWN = MODES // GROUPS
 ROWS = KEPT // SLABS
+HALF = NG // 2
 PARTS = NG // DEVS
 QUART = NG // 4
 FACTOR = 1.0 / math.sqrt(NG)
@@ -54,14 +55,22 @@
 
 def y_tables():
     waves = np.arange(KEPT)
-    points = np.arange(NG)
-    cos, sin = circle(waves[:, None] * points[None, :])
+    cos, sin = circle(waves[:, None] * np.arange(HALF)[None, :])
     weights = np.where(waves == 0, 1.0, 2.0).astype(np.float32)[:, None]
-    ahead = np.stack([(weights * cos).reshape(SLABS, ROWS, NG), (-weights * sin).reshape(SLABS, ROWS, NG)], axis=1)
-    ahead = ahead.reshape(2 * KEPT, NG).astype(ml_dtypes.bfloat16)
-    back = np.stack([cos.T.reshape(NG, SLABS, ROWS), -sin.T.reshape(NG, SLABS, ROWS)], axis=2)
-    back = back[:, :LIVE].reshape(NG, LIVE * 2 * ROWS).astype(ml_dtypes.bfloat16)
-    return ahead, back
+    split = (SLABS // 8, 2, 4, ROWS // 2, 2, HALF)
+    ahead = np.stack([(weights * cos).reshape(split), (-weights * sin).reshape(split)], axis=6)
+    ahead = ahead.transpose(4, 0, 2, 6, 3, 1, 5).reshape(2, KEPT, HALF)
+    back = np.stack([cos.reshape(split), -sin.reshape(split)], axis=6)[: LIVE // 8]
+    back = back.transpose(4, 5, 0, 2, 6, 3, 1).reshape(2, HALF, LIVE * ROWS)
+    return ahead.astype(ml_dtypes.bfloat16), back.astype(ml_dtypes.bfloat16)
+
+
+def even_odd(first, second):
+    lane = lax.broadcasted_iota(jnp.int32, first.shape, 1)
+    return (
+        jnp.where(lane % 2 == 0, first, pltpu.roll(second, 1, 1)),
+        jnp.where(lane % 2 == 0, pltpu.roll(first, 127, 1), second),
+    )
 
 
 def lane_masks():
@@ -181,9 +190,9 @@
 
 
 def points_kernel(
-    in_ref, ahead_ref, triple_ref, back_ref, out_ref, wide_ref, left_ref, phys_ref, flux_ref, half_ref, send_ref
+    in_ref, ahead_ref, triple_ref, back_ref, out_ref, wide_ref, left_ref, phys_ref, keep_ref, flux_ref, half_ref, send_ref
 ):
-    chunk = 512
+    chunk = HALF
     tall = 24 * GROUPS
     masks = lane_masks()
     span = SLABS * OUT
@@ -193,23 +202,29 @@
     def gather(pair, carry):
         for side in range(2):
             wide_ref[side, :span] = in_ref[pl.ds(pl.multiple_of((pair * 2 + side) * span, span), span)].astype(F32)
-        for quad in range(SLABS // 4):
-            sides = []
-            for side in range(2):
-                blocks = [wide_ref[side, (quad * 4 + j) * OUT : (quad * 4 + j) * OUT + 24] for j in range(4)]
-                parts = []
-                for part in range(PARTS):
-                    mixed = pick(masks, [blocks[(slot - part) % 4] for slot in range(4)])
-                    parts.append(pltpu.roll(mixed, 128 - 32 * part, 1) if part else mixed)
-                sides.append(parts)
+        for eight in range(SLABS // 8):
+            quads = []
+            for quad in (2 * eight, 2 * eight + 1):
+                blocks = []
+                for j in range(4):
+                    at = (quad * 4 + j) * OUT
+                    blocks.append(jnp.concatenate([wide_ref[side, at : at + 24] for side in range(2)], axis=0).astype(BF))
+                quads.append(blocks)
             for part in range(PARTS):
-                both = jnp.concatenate([sides[0][part], sides[1][part]], axis=0)
+                mixed = []
+                for blocks in quads:
+                    one = pick(masks, [blocks[(slot - part) % 4] for slot in range(4)])
+                    mixed.append(pltpu.roll(one, 128 - 32 * part, 1) if part else one)
                 rows = pl.ds(pl.multiple_of(part * tall + pair * 48, 48), 48)
-                left_ref[rows, quad * 128 : (quad + 1) * 128] = both.astype(BF)
+                for parity, both in enumerate(even_odd(*mixed)):
+                    left_ref[parity, rows, eight * 128 : (eight + 1) * 128] = both.astype(BF)
         return carry
 
     lax.fori_loop(0, GROUPS // 2, gather, 0, unroll=True)
-    phys_ref[...] = jnp.dot(left_ref[...], ahead_ref[...], preferred_element_type=F32) * FACTOR
+    even = jnp.dot(left_ref[0], ahead_ref[0], preferred_element_type=F32) * FACTOR
+    odd = jnp.dot(left_ref[1], ahead_ref[1], preferred_element_type=F32) * FACTOR
+    phys_ref[:, :HALF] = even + odd
+    phys_ref[:, HALF:] = even - odd
 
     def line(part, carry):
         base = pl.multiple_of(part * tall, tall)
@@ -234,21 +249,30 @@
             for group in range(GROUPS):
                 own = slice(group * OWN, (group + 1) * OWN)
                 both = jnp.concatenate([sum_x[own], sum_y[own], jnp.zeros((2, chunk), F32)], axis=0)
-                flux_ref[pl.ds(pl.multiple_of((part * GROUPS + group) * 16, 16), 16), lanes] = both.astype(BF)
+                if step == 0:
+                    keep_ref[group * 16 : (group + 1) * 16] = both
+                else:
+                    first = keep_ref[group * 16 : (group + 1) * 16]
+                    rows = pl.ds(pl.multiple_of((part * GROUPS + group) * 16, 16), 16)
+                    flux_ref[0, rows] = (first + both).astype(BF)
+                    flux_ref[1, rows] = (first - both).astype(BF)
         return carry
 
     lax.fori_loop(0, PARTS, line, 0)
-    half_ref[...] = jnp.dot(flux_ref[...], back_ref[...], preferred_element_type=F32) * FACTOR
-    for quad in range(LIVE // 4):
-        rolled = []
+    for parity in range(2):
+        half_ref[parity] = jnp.dot(flux_ref[parity], back_ref[parity], preferred_element_type=F32) * FACTOR
+    for eight in range(LIVE // 8):
+        quads = ([], [])
         for part in range(PARTS):
-            block = half_ref[part * 128 : (part + 1) * 128, quad * 128 : (quad + 1) * 128]
-            rolled.append(pltpu.roll(block, 32 * part, 1) if part else block)
-        for j in range(4):
-            block = pick(masks, [rolled[(slot - j) % 4] for slot in range(4)])
-            for group in range(GROUPS):
-                at = (group * SLABS + quad * 4 + j) * HOME
-                send_ref[at : at + HOME] = block[group * 16 : group * 16 + HOME]
+            rows, lanes = slice(part * 128, (part + 1) * 128), slice(eight * 128, (eight + 1) * 128)
+            for rolled, block in zip(quads, even_odd(half_ref[0, rows, lanes].astype(BF), half_ref[1, rows, lanes].astype(BF))):
+                rolled.append(pltpu.roll(block, 32 * part, 1) if part else block)
+        for quad, rolled in enumerate(quads):
+            for j in range(4):
+                block = pick(masks, [rolled[(slot - j) % 4] for slot in range(4)]).astype(F32)
+                for group in range(GROUPS):
+                    at = (group * SLABS + eight * 8 + quad * 4 + j) * HOME
+                    send_ref[at : at + HOME] = block[group * 16 : group * 16 + HOME]
     for group in range(GROUPS):
         at = (group * SLABS + LIVE) * HOME
         send_ref[at : at + (SLABS - LIVE) * HOME] = jnp.zeros(((SLABS - LIVE) * HOME, 128), F32)
@@ -352,10 +376,11 @@
         jax.ShapeDtypeStruct((DEVS * HOME, 128), BF),
         [
             pltpu.VMEM((2, SLABS * OUT + 8, 128), F32),
-            pltpu.VMEM((PARTS * 24 * GROUPS, NG), BF),
+            pltpu.VMEM((2, PARTS * 24 * GROUPS, KEPT), BF),
             pltpu.VMEM((PARTS * 24 * GROUPS, NG), F32),
-            pltpu.VMEM((PARTS * 16 * GROUPS, NG), BF),
-            pltpu.VMEM((PARTS * 16 * GROUPS, LIVE * 32), F32),
+            pltpu.VMEM((16 * GROUPS, HALF), F32),
+            pltpu.VMEM((2, PARTS * 16 * GROUPS, HALF), BF),
+            pltpu.VMEM((2, PARTS * 16 * GROUPS, LIVE * ROWS), F32),
             pltpu.VMEM((DEVS * HOME, 128), F32),
         ],
         [vmem] * 4,

time: 110 us -> 109 us (level)
  Pallas kernels: 19.5 us -> 18.2 us
    pallas_call x1, Pallas kernels: 12.4 us -> 11.3 us  [shards(): call(points_kernel, jax.ShapeDtypeStruct((DEVS * HOME, 128), BF), [pltpu....]
where the time goes in v6:
time: 109 us
  blocking collectives  89.5 us (82%)
  Pallas kernels  18.2 us (17%)
    all_to_all x2, blocking collectives, exchange(): lax.all_to_all(blocks, ('mode', 'grid'), split_axis=0, concat_axis=0, til...  89.5 us
    pallas_call x1, Pallas kernels, shards(): call(points_kernel, jax.ShapeDtypeStruct((DEVS * HOME, 128), BF), [pltpu....  11.3 us
    pallas_call x1, Pallas kernels, shards(): call(columns_kernel, jax.ShapeDtypeStruct((DEVS * OUT, 128), BF), [pltpu....  4.7 us
    pallas_call x1, Pallas kernels, shards(): call(update_kernel, (new, new), [pltpu.VMEM((DEVS * HOME, 128), F32), plt...  2.26 us

profile of v6, /device:TPU:1, one launch (start us, length us, event | category | flops | bytes accessed | tf_op | source)
XLA Modules:
  0.0 108.5 jit_solution(7083423542380653057)
XLA Ops:
  0.6 4.7 %shard_map.104 = bf16[5632,128]{1,0:T(8,128)(2,1)} custom-call(f32[7,16,1024]{2,1,0:T(8,128)} %re_ref.1, f32[7,16,1024]{2,1,0:T(8,128)} %im_ref.1, bf16[4,256,512]{2,1,0:T(8,128)(2,1)} %constant.8.clone.table_hbm), custom_call_target="tpu_custom_call" | custom-call | flops 1000000000 | bytes 4194304 | tf_op jit(solution)/shard_map/pallas_call | solution.py:355
  5.3 0.0 copy-start.5
  5.4 0.0 copy-start.6
  5.4 0.0 copy-start.7
  5.4 55.1 %all_to_all.10 = bf16[256,11,2,128]{3,2,1,0:T(2,128)(2,1)S(1)} all-to-all(bf16[256,11,2,128]{3,2,1,0:T(2,128)(2,1)} %bitcast.9), channel_id=1, replica_groups=mesh['mode'=8,'grid'=32] {'mode','grid'}, dimensions={0} | all-to-all | bytes 2883584 | tf_op jit(solution)/shard_map/all_to_all | solution.py:345
  60.5 0.0 copy-done.5
  60.5 0.0 copy-done.6
  60.5 0.0 copy-done.7
  60.5 0.0 copy-start
  60.5 11.3 %shard_map.105 = bf16[3584,128]{1,0:T(8,128)(2,1)S(1)} custom-call(bf16[5632,128]{1,0:T(8,128)(2,1)S(1)} %bitcast.6, bf16[2,512,512]{2,1,0:T(8,128)(2,1)S(1)} %copy-done.6, bf16[3136,56]{1,0:T(8,128)(2,1)S(1)} %bitcast.8, bf16[2,512,384]{2,1,0:T(8,128)(2,1)S(1)} %copy-done.7), custom_call_target="tpu_custom_call" | custom-call | flops 10000000000 | bytes 4194304 | tf_op jit(solution)/shard_map/pallas_call | solution.py:374
  71.8 0.0 copy-start.1
  71.8 0.0 copy-start.2
  71.8 0.0 copy-start.3
  71.8 0.0 copy-start.4
  71.9 34.4 %all_to_all.11 = bf16[256,7,2,128]{3,2,1,0:T(2,128)(2,1)S(1)} all-to-all(bf16[256,7,2,128]{3,2,1,0:T(2,128)(2,1)S(1)} %bitcast.7), channel_id=1, replica_groups=mesh['mode'=8,'grid'=32] {'mode','grid'}, dimensions={0} | all-to-all | bytes 1835008 | tf_op jit(solution)/shard_map/all_to_all | solution.py:345
  106.2 0.0 copy-done
  106.2 0.0 copy-done.1
  106.2 0.0 copy-done.2
  106.3 0.0 copy-done.3
  106.3 0.0 copy-done.4
  106.3 2.3 %shard_map.106 = (f32[7,16,1024]{2,1,0:T(8,128)}, f32[7,16,1024]{2,1,0:T(8,128)}) custom-call(bf16[3584,128]{1,0:T(8,128)(2,1)S(1)} %bitcast.5, bf16[4,512,512]{2,1,0:T(8,128)(2,1)S(1)} %copy-done, f32[7,16,1024]{2,1,0:T(8,128)S(1)} %copy-done.1, f32[7,16,1024]{2,1,0:T(8,128)S(1)} %copy-done.2, f32[7,16,1024]{2,1,0:T(8,128)S(1)} %copy-done.3, ...), custom_call_target="tpu_custom_call" | custom-call | flops 1000000000 | bytes 4194304 | tf_op jit(solution)/shard_map/pallas_call | solution.py:391
Async XLA Ops:
  5.3 55.2 %copy-start.5 = (bf16[56,56,56]{2,1,0:T(8,128)(2,1)S(1)}, bf16[56,56,56]{2,1,0:T(8,128)(2,1)}, u32[]{:S(2)}) copy-start(bf16[56,56,56]{2,1,0:T(8,128)(2,1)} %param.13) | copy-start | bytes 1053700
  5.4 55.2 %copy-start.6 = (bf16[2,512,512]{2,1,0:T(8,128)(2,1)S(1)}, bf16[2,512,512]{2,1,0:T(8,128)(2,1)}, u32[]{:S(2)}) copy-start(bf16[2,512,512]{2,1,0:T(8,128)(2,1)} %constant.9.clone.ahead_ref) | copy-start | bytes 3145732
  5.4 55.1 %copy-start.7 = (bf16[2,512,384]{2,1,0:T(8,128)(2,1)S(1)}, bf16[2,512,384]{2,1,0:T(8,128)(2,1)}, u32[]{:S(2)}) copy-start(bf16[2,512,384]{2,1,0:T(8,128)(2,1)} %constant.10.clone.back_ref) | copy-start | bytes 2359300
  60.5 45.7 %copy-start = (bf16[4,512,512]{2,1,0:T(8,128)(2,1)S(1)}, bf16[4,512,512]{2,1,0:T(8,128)(2,1)}, u32[]{:S(2)}) copy-start(bf16[4,512,512]{2,1,0:T(8,128)(2,1)} %constant.11.clone.table_ref) | copy-start | bytes 6291460
  71.8 34.4 %copy-start.1 = (f32[7,16,1024]{2,1,0:T(8,128)S(1)}, f32[7,16,1024]{2,1,0:T(8,128)}, u32[]{:S(2)}) copy-start(f32[7,16,1024]{2,1,0:T(8,128)} %re_ref.1) | copy-start | bytes 1376260
  71.8 34.4 %copy-start.2 = (f32[7,16,1024]{2,1,0:T(8,128)S(1)}, f32[7,16,1024]{2,1,0:T(8,128)}, u32[]{:S(2)}) copy-start(f32[7,16,1024]{2,1,0:T(8,128)} %im_ref.1) | copy-start | bytes 1376260
  71.8 34.4 %copy-start.3 = (f32[7,16,1024]{2,1,0:T(8,128)S(1)}, f32[7,16,1024]{2,1,0:T(8,128)}, u32[]{:S(2)}) copy-start(f32[7,16,1024]{2,1,0:T(8,128)} %base_re_ref.1) | copy-start | bytes 1376260
  71.8 34.4 %copy-start.4 = (f32[7,16,1024]{2,1,0:T(8,128)S(1)}, f32[7,16,1024]{2,1,0:T(8,128)}, u32[]{:S(2)}) copy-start(f32[7,16,1024]{2,1,0:T(8,128)} %base_im_ref.1) | copy-start | bytes 1376260

commit v7 on v6

--- a/solution.py
+++ b/solution.py
@@ -38,6 +38,10 @@
     return np.cos(angles), np.sin(angles)
 
 
+def scaled(table):
+    return (table.astype(ml_dtypes.bfloat16).astype(np.float32) * np.float32(FACTOR)).astype(ml_dtypes.bfloat16)
+
+
 def x_tables():
     ahead, back = [], []
     short = np.arange(QUART)
@@ -47,10 +51,7 @@
         ahead.append(np.block([[cos, sin]]))
         cos, sin = circle(points[:, None] * short[None, :])
         back.append(np.block([[cos, -sin], [sin, cos]]))
-    return (
-        np.stack(ahead).astype(ml_dtypes.bfloat16),
-        np.stack(back).astype(ml_dtypes.bfloat16),
-    )
+    return scaled(np.stack(ahead)), scaled(np.stack(back))
 
 
 def y_tables():
@@ -62,7 +63,7 @@
     ahead = ahead.transpose(4, 0, 2, 6, 3, 1, 5).reshape(2, KEPT, HALF)
     back = np.stack([cos.reshape(split), -sin.reshape(split)], axis=6)[: LIVE // 8]
     back = back.transpose(4, 5, 0, 2, 6, 3, 1).reshape(2, HALF, LIVE * ROWS)
-    return ahead.astype(ml_dtypes.bfloat16), back.astype(ml_dtypes.bfloat16)
+    return scaled(ahead), scaled(back)
 
 
 def even_odd(first, second):
@@ -161,9 +162,7 @@
         tables[part].wait()
         table_ref[part, QUART:, :QUART] = -table_ref[part, :QUART, QUART:]
         table_ref[part, QUART:, QUART:] = table_ref[part, :QUART, :QUART]
-        prod_ref[part] = (
-            jnp.dot(left_ref[part], table_ref[part], preferred_element_type=F32) * FACTOR
-        )
+        prod_ref[part] = jnp.dot(left_ref[part], table_ref[part], preferred_element_type=F32)
     slots = slots_of(slab)
     sends = []
     for side in range(2):
@@ -178,7 +177,7 @@
                 axis=0,
             )
             turn_ref[pl.ds(at, half, stride=OUT), :] = block.T
-        send_ref[side] = turn_ref[...].astype(BF)
+        send_ref[side] = turn_ref[: half * OUT].astype(BF)
         sends.append(
             pltpu.make_async_copy(
                 send_ref.at[side], out_hbm.at[pl.ds(side * half * OUT, half * OUT)], sems.at[2 * OWN + PARTS + side]
@@ -197,7 +196,7 @@
     masks = lane_masks()
     span = SLABS * OUT
     for side in range(2):
-        wide_ref[side, span:] = jnp.zeros((8, 128), F32)
+        wide_ref[side, span:] = jnp.zeros((16, 128), F32)
 
     def gather(pair, carry):
         for side in range(2):
@@ -221,8 +220,8 @@
         return carry
 
     lax.fori_loop(0, GROUPS // 2, gather, 0, unroll=True)
-    even = jnp.dot(left_ref[0], ahead_ref[0], preferred_element_type=F32) * FACTOR
-    odd = jnp.dot(left_ref[1], ahead_ref[1], preferred_element_type=F32) * FACTOR
+    even = jnp.dot(left_ref[0], ahead_ref[0], preferred_element_type=F32)
+    odd = jnp.dot(left_ref[1], ahead_ref[1], preferred_element_type=F32)
     phys_ref[:, :HALF] = even + odd
     phys_ref[:, HALF:] = even - odd
 
@@ -260,7 +259,7 @@
 
     lax.fori_loop(0, PARTS, line, 0)
     for parity in range(2):
-        half_ref[parity] = jnp.dot(flux_ref[parity], back_ref[parity], preferred_element_type=F32) * FACTOR
+        half_ref[parity] = jnp.dot(flux_ref[parity], back_ref[parity], preferred_element_type=F32)
     for eight in range(LIVE // 8):
         quads = ([], [])
         for part in range(PARTS):
@@ -276,25 +275,23 @@
     for group in range(GROUPS):
         at = (group * SLABS + LIVE) * HOME
         send_ref[at : at + (SLABS - LIVE) * HOME] = jnp.zeros(((SLABS - LIVE) * HOME, 128), F32)
-    out_ref[...] = send_ref[...].astype(BF)
+    out_ref[...] = send_ref[: DEVS * HOME].astype(BF)
 
 
 def update_kernel(
     in_ref, table_ref, re_ref, im_ref, base_re_ref, base_im_ref, new_re, new_im, wide_ref, left_ref, prod_ref, new_re_ref, new_im_ref, sems
 ):
-    wide_ref[...] = in_ref[...].astype(F32)
+    wide_ref[: DEVS * HOME] = in_ref[...].astype(F32)
     slab = lax.axis_index("grid")
     slots = slots_of(slab)
     for at in range(2 * OWN):
-        block = wide_ref[pl.ds(at, DEVS, stride=HOME), :].T.astype(BF)
+        block = wide_ref[pl.ds(at, DEVS, stride=HOME), :].astype(BF).T
         for slot in range(PARTS):
             for c in range(2):
                 row = (slot * 2 + c) * ROWS
                 left_ref[slots[slot], at * ROWS : (at + 1) * ROWS, c * QUART : (c + 1) * QUART] = block[row : row + ROWS]
     for part in range(PARTS):
-        prod_ref[part] = (
-            jnp.dot(left_ref[part], table_ref[part], preferred_element_type=F32) * FACTOR
-        )
+        prod_ref[part] = jnp.dot(left_ref[part], table_ref[part], preferred_element_type=F32)
     along_y, along_x = waves_of(slab * ROWS)
     wave_sq = along_y * along_y + along_x * along_x
     keep = (jnp.abs(along_x) * 3.0 < NG) & (along_y * 3.0 < NG)
@@ -361,7 +358,7 @@
             pltpu.VMEM((PARTS, 2 * QUART, 2 * QUART), BF),
             pltpu.VMEM((PARTS, count * ROWS, 2 * QUART), BF),
             pltpu.VMEM((PARTS, count * ROWS, 2 * QUART), F32),
-            pltpu.VMEM((DEVS // 2 * OUT, 128), F32),
+            pltpu.VMEM((DEVS // 2 * OUT + 32, 128), F32),
             pltpu.VMEM((2, DEVS // 2 * OUT, 128), BF),
             pltpu.SemaphoreType.DMA((2 * OWN + PARTS + 2,)),
         ],
@@ -375,13 +372,13 @@
         points_kernel,
         jax.ShapeDtypeStruct((DEVS * HOME, 128), BF),
         [
-            pltpu.VMEM((2, SLABS * OUT + 8, 128), F32),
+            pltpu.VMEM((2, SLABS * OUT + 16, 128), F32),
             pltpu.VMEM((2, PARTS * 24 * GROUPS, KEPT), BF),
             pltpu.VMEM((PARTS * 24 * GROUPS, NG), F32),
             pltpu.VMEM((16 * GROUPS, HALF), F32),
             pltpu.VMEM((2, PARTS * 16 * GROUPS, HALF), BF),
             pltpu.VMEM((2, PARTS * 16 * GROUPS, LIVE * ROWS), F32),
-            pltpu.VMEM((DEVS * HOME, 128), F32),
+            pltpu.VMEM((DEVS * HOME + 16, 128), F32),
         ],
         [vmem] * 4,
         10_000_000_000,
@@ -392,7 +389,7 @@
         update_kernel,
         (new, new),
         [
-            pltpu.VMEM((DEVS * HOME, 128), F32),
+            pltpu.VMEM((DEVS * HOME + 16, 128), F32),
             pltpu.VMEM((PARTS, 2 * OWN * ROWS, 2 * QUART), BF),
             pltpu.VMEM((PARTS, 2 * OWN * ROWS, 2 * QUART), F32),
             pltpu.VMEM(base_re.shape, F32),

time: 109 us -> 108 us (level)
  no operation moved by 1% of the time
where the time goes in v7:
time: 108 us
  blocking collectives  89.5 us (83%)
  Pallas kernels  17.7 us (16%)
    all_to_all x2, blocking collectives, exchange(): lax.all_to_all(blocks, ('mode', 'grid'), split_axis=0, concat_axis=0, til...  89.5 us
    pallas_call x1, Pallas kernels, shards(): call(points_kernel, jax.ShapeDtypeStruct((DEVS * HOME, 128), BF), [pltpu....  10.9 us
    pallas_call x1, Pallas kernels, shards(): call(columns_kernel, jax.ShapeDtypeStruct((DEVS * OUT, 128), BF), [pltpu....  4.72 us

profile of v7, /device:TPU:1, one launch (start us, length us, event | category | flops | bytes accessed | tf_op | source)
XLA Modules:
  0.0 108.0 jit_solution(15099467049491433317)
XLA Ops:
  0.6 4.7 %shard_map.104 = bf16[5632,128]{1,0:T(8,128)(2,1)} custom-call(f32[7,16,1024]{2,1,0:T(8,128)} %re_ref.1, f32[7,16,1024]{2,1,0:T(8,128)} %im_ref.1, bf16[4,256,512]{2,1,0:T(8,128)(2,1)} %constant.8.clone.table_hbm), custom_call_target="tpu_custom_call" | custom-call | flops 1000000000 | bytes 4194304 | tf_op jit(solution)/shard_map/pallas_call | solution.py:352
  5.4 0.0 copy-start.5
  5.4 0.0 copy-start.6
  5.4 0.0 copy-start.7
  5.4 55.1 %all_to_all.10 = bf16[256,11,2,128]{3,2,1,0:T(2,128)(2,1)S(1)} all-to-all(bf16[256,11,2,128]{3,2,1,0:T(2,128)(2,1)} %bitcast.9), channel_id=1, replica_groups=mesh['mode'=8,'grid'=32] {'mode','grid'}, dimensions={0} | all-to-all | bytes 2883584 | tf_op jit(solution)/shard_map/all_to_all | solution.py:342
  60.5 0.0 copy-done.5
  60.5 0.0 copy-done.6
  60.5 0.0 copy-done.7
  60.5 0.0 copy-start
  60.5 10.9 %shard_map.105 = bf16[3584,128]{1,0:T(8,128)(2,1)S(1)} custom-call(bf16[5632,128]{1,0:T(8,128)(2,1)S(1)} %bitcast.6, bf16[2,512,512]{2,1,0:T(8,128)(2,1)S(1)} %copy-done.6, bf16[3136,56]{1,0:T(8,128)(2,1)S(1)} %bitcast.8, bf16[2,512,384]{2,1,0:T(8,128)(2,1)S(1)} %copy-done.7), custom_call_target="tpu_custom_call" | custom-call | flops 10000000000 | bytes 4194304 | tf_op jit(solution)/shard_map/pallas_call | solution.py:371
  71.4 0.0 copy-start.1
  71.4 0.0 copy-start.2
  71.4 0.0 copy-start.3
  71.4 0.0 copy-start.4
  71.5 34.4 %all_to_all.11 = bf16[256,7,2,128]{3,2,1,0:T(2,128)(2,1)S(1)} all-to-all(bf16[256,7,2,128]{3,2,1,0:T(2,128)(2,1)S(1)} %bitcast.7), channel_id=1, replica_groups=mesh['mode'=8,'grid'=32] {'mode','grid'}, dimensions={0} | all-to-all | bytes 1835008 | tf_op jit(solution)/shard_map/all_to_all | solution.py:342
  105.9 0.0 copy-done
  105.9 0.0 copy-done.1
  105.9 0.0 copy-done.2
  105.9 0.0 copy-done.3
  105.9 0.0 copy-done.4
  105.9 2.2 %shard_map.106 = (f32[7,16,1024]{2,1,0:T(8,128)}, f32[7,16,1024]{2,1,0:T(8,128)}) custom-call(bf16[3584,128]{1,0:T(8,128)(2,1)S(1)} %bitcast.5, bf16[4,512,512]{2,1,0:T(8,128)(2,1)S(1)} %copy-done, f32[7,16,1024]{2,1,0:T(8,128)S(1)} %copy-done.1, f32[7,16,1024]{2,1,0:T(8,128)S(1)} %copy-done.2, f32[7,16,1024]{2,1,0:T(8,128)S(1)} %copy-done.3, ...), custom_call_target="tpu_custom_call" | custom-call | flops 1000000000 | bytes 4194304 | tf_op jit(solution)/shard_map/pallas_call | solution.py:388
Async XLA Ops:
  5.4 55.2 %copy-start.5 = (bf16[56,56,56]{2,1,0:T(8,128)(2,1)S(1)}, bf16[56,56,56]{2,1,0:T(8,128)(2,1)}, u32[]{:S(2)}) copy-start(bf16[56,56,56]{2,1,0:T(8,128)(2,1)} %param.13) | copy-start | bytes 1053700
  5.4 55.1 %copy-start.6 = (bf16[2,512,512]{2,1,0:T(8,128)(2,1)S(1)}, bf16[2,512,512]{2,1,0:T(8,128)(2,1)}, u32[]{:S(2)}) copy-start(bf16[2,512,512]{2,1,0:T(8,128)(2,1)} %constant.9.clone.ahead_ref) | copy-start | bytes 3145732
  5.4 55.1 %copy-start.7 = (bf16[2,512,384]{2,1,0:T(8,128)(2,1)S(1)}, bf16[2,512,384]{2,1,0:T(8,128)(2,1)}, u32[]{:S(2)}) copy-start(bf16[2,512,384]{2,1,0:T(8,128)(2,1)} %constant.10.clone.back_ref) | copy-start | bytes 2359300
  60.5 45.3 %copy-start = (bf16[4,512,512]{2,1,0:T(8,128)(2,1)S(1)}, bf16[4,512,512]{2,1,0:T(8,128)(2,1)}, u32[]{:S(2)}) copy-start(bf16[4,512,512]{2,1,0:T(8,128)(2,1)} %constant.11.clone.table_ref) | copy-start | bytes 6291460
  71.4 34.5 %copy-start.1 = (f32[7,16,1024]{2,1,0:T(8,128)S(1)}, f32[7,16,1024]{2,1,0:T(8,128)}, u32[]{:S(2)}) copy-start(f32[7,16,1024]{2,1,0:T(8,128)} %re_ref.1) | copy-start | bytes 1376260
  71.4 34.4 %copy-start.2 = (f32[7,16,1024]{2,1,0:T(8,128)S(1)}, f32[7,16,1024]{2,1,0:T(8,128)}, u32[]{:S(2)}) copy-start(f32[7,16,1024]{2,1,0:T(8,128)} %im_ref.1) | copy-start | bytes 1376260
  71.4 34.4 %copy-start.3 = (f32[7,16,1024]{2,1,0:T(8,128)S(1)}, f32[7,16,1024]{2,1,0:T(8,128)}, u32[]{:S(2)}) copy-start(f32[7,16,1024]{2,1,0:T(8,128)} %base_re_ref.1) | copy-start | bytes 1376260
  71.4 34.4 %copy-start.4 = (f32[7,16,1024]{2,1,0:T(8,128)S(1)}, f32[7,16,1024]{2,1,0:T(8,128)}, u32[]{:S(2)}) copy-start(f32[7,16,1024]{2,1,0:T(8,128)} %base_im_ref.1) | copy-start | bytes 1376260

commit v8 on v7

--- a/solution.py
+++ b/solution.py
@@ -162,21 +162,25 @@
         tables[part].wait()
         table_ref[part, QUART:, :QUART] = -table_ref[part, :QUART, QUART:]
         table_ref[part, QUART:, QUART:] = table_ref[part, :QUART, :QUART]
-        prod_ref[part] = jnp.dot(left_ref[part], table_ref[part], preferred_element_type=F32)
     slots = slots_of(slab)
     sends = []
     for side in range(2):
+        for part in range(PARTS):
+            own = jnp.concatenate(
+                [table_ref[part, :, c * QUART + side * half : c * QUART + (side + 1) * half] for c in range(2)], axis=1
+            )
+            prod_ref[side, part] = jnp.dot(left_ref[part], own, preferred_element_type=F32)
         for at in range(count):
             rows = slice(at * ROWS, (at + 1) * ROWS)
             block = jnp.concatenate(
                 [
-                    prod_ref[slots[slot], rows, c * QUART + side * half : c * QUART + (side + 1) * half]
+                    prod_ref[side, slots[slot], rows, c * half : (c + 1) * half]
                     for slot in range(PARTS)
                     for c in range(2)
                 ],
                 axis=0,
             )
-            turn_ref[pl.ds(at, half, stride=OUT), :] = block.T
+            turn_ref[pl.ds(at, half, stride=OUT), :] = block.astype(BF).T.astype(F32)
         send_ref[side] = turn_ref[: half * OUT].astype(BF)
         sends.append(
             pltpu.make_async_copy(
@@ -357,7 +361,7 @@
             pltpu.VMEM((OWN, ROWS, NG), F32),
             pltpu.VMEM((PARTS, 2 * QUART, 2 * QUART), BF),
             pltpu.VMEM((PARTS, count * ROWS, 2 * QUART), BF),
-            pltpu.VMEM((PARTS, count * ROWS, 2 * QUART), F32),
+            pltpu.VMEM((2, PARTS, count * ROWS, QUART), F32),
             pltpu.VMEM((DEVS // 2 * OUT + 32, 128), F32),
             pltpu.VMEM((2, DEVS // 2 * OUT, 128), BF),
             pltpu.SemaphoreType.DMA((2 * OWN + PARTS + 2,)),

time: 108 us -> 108 us (level)
  no operation moved by 1% of the time
where the time goes in v8:
time: 108 us; the launch traced here: 107 us
  blocking collectives  89.5 us (83%)
  Pallas kernels  17.1 us (16%)
    all_to_all x2, blocking collectives, exchange(): lax.all_to_all(blocks, ('mode', 'grid'), split_axis=0, concat_axis=0, til...  89.5 us
    pallas_call x1, Pallas kernels, shards(): call(points_kernel, jax.ShapeDtypeStruct((DEVS * HOME, 128), BF), [pltpu....  10.9 us
    pallas_call x1, Pallas kernels, shards(): call(columns_kernel, jax.ShapeDtypeStruct((DEVS * OUT, 128), BF), [pltpu....  4.09 us

profile of v8, /device:TPU:1, one launch (start us, length us, event | category | flops | bytes accessed | tf_op | source)
XLA Modules:
  0.0 107.4 jit_solution(13559905651877397908)
XLA Ops:
  0.6 4.1 %shard_map.104 = bf16[5632,128]{1,0:T(8,128)(2,1)} custom-call(f32[7,16,1024]{2,1,0:T(8,128)} %re_ref.1, f32[7,16,1024]{2,1,0:T(8,128)} %im_ref.1, bf16[4,256,512]{2,1,0:T(8,128)(2,1)} %constant.8.clone.table_hbm), custom_call_target="tpu_custom_call" | custom-call | flops 1000000000 | bytes 4194304 | tf_op jit(solution)/shard_map/pallas_call | solution.py:356
  4.7 0.0 copy-start.5
  4.7 0.0 copy-start.6
  4.8 0.0 copy-start.7
  4.8 55.1 %all_to_all.10 = bf16[256,11,2,128]{3,2,1,0:T(2,128)(2,1)S(1)} all-to-all(bf16[256,11,2,128]{3,2,1,0:T(2,128)(2,1)} %bitcast.9), channel_id=1, replica_groups=mesh['mode'=8,'grid'=32] {'mode','grid'}, dimensions={0} | all-to-all | bytes 2883584 | tf_op jit(solution)/shard_map/all_to_all | solution.py:346
  59.9 0.0 copy-done.5
  59.9 0.0 copy-done.6
  59.9 0.0 copy-done.7
  59.9 0.0 copy-start
  59.9 10.9 %shard_map.105 = bf16[3584,128]{1,0:T(8,128)(2,1)S(1)} custom-call(bf16[5632,128]{1,0:T(8,128)(2,1)S(1)} %bitcast.6, bf16[2,512,512]{2,1,0:T(8,128)(2,1)S(1)} %copy-done.6, bf16[3136,56]{1,0:T(8,128)(2,1)S(1)} %bitcast.8, bf16[2,512,384]{2,1,0:T(8,128)(2,1)S(1)} %copy-done.7), custom_call_target="tpu_custom_call" | custom-call | flops 10000000000 | bytes 4194304 | tf_op jit(solution)/shard_map/pallas_call | solution.py:375
  70.8 0.0 copy-start.1
  70.8 0.0 copy-start.2
  70.8 0.0 copy-start.3
  70.8 0.0 copy-start.4
  70.8 34.4 %all_to_all.11 = bf16[256,7,2,128]{3,2,1,0:T(2,128)(2,1)S(1)} all-to-all(bf16[256,7,2,128]{3,2,1,0:T(2,128)(2,1)S(1)} %bitcast.7), channel_id=1, replica_groups=mesh['mode'=8,'grid'=32] {'mode','grid'}, dimensions={0} | all-to-all | bytes 1835008 | tf_op jit(solution)/shard_map/all_to_all | solution.py:346
  105.2 0.0 copy-done
  105.2 0.0 copy-done.1
  105.2 0.0 copy-done.2
  105.2 0.0 copy-done.3
  105.2 0.0 copy-done.4
  105.3 2.2 %shard_map.106 = (f32[7,16,1024]{2,1,0:T(8,128)}, f32[7,16,1024]{2,1,0:T(8,128)}) custom-call(bf16[3584,128]{1,0:T(8,128)(2,1)S(1)} %bitcast.5, bf16[4,512,512]{2,1,0:T(8,128)(2,1)S(1)} %copy-done, f32[7,16,1024]{2,1,0:T(8,128)S(1)} %copy-done.1, f32[7,16,1024]{2,1,0:T(8,128)S(1)} %copy-done.2, f32[7,16,1024]{2,1,0:T(8,128)S(1)} %copy-done.3, ...), custom_call_target="tpu_custom_call" | custom-call | flops 1000000000 | bytes 4194304 | tf_op jit(solution)/shard_map/pallas_call | solution.py:392
Async XLA Ops:
  4.7 55.2 %copy-start.5 = (bf16[56,56,56]{2,1,0:T(8,128)(2,1)S(1)}, bf16[56,56,56]{2,1,0:T(8,128)(2,1)}, u32[]{:S(2)}) copy-start(bf16[56,56,56]{2,1,0:T(8,128)(2,1)} %param.13) | copy-start | bytes 1053700
  4.7 55.1 %copy-start.6 = (bf16[2,512,512]{2,1,0:T(8,128)(2,1)S(1)}, bf16[2,512,512]{2,1,0:T(8,128)(2,1)}, u32[]{:S(2)}) copy-start(bf16[2,512,512]{2,1,0:T(8,128)(2,1)} %constant.9.clone.ahead_ref) | copy-start | bytes 3145732
  4.8 55.1 %copy-start.7 = (bf16[2,512,384]{2,1,0:T(8,128)(2,1)S(1)}, bf16[2,512,384]{2,1,0:T(8,128)(2,1)}, u32[]{:S(2)}) copy-start(bf16[2,512,384]{2,1,0:T(8,128)(2,1)} %constant.10.clone.back_ref) | copy-start | bytes 2359300
  59.9 45.3 %copy-start = (bf16[4,512,512]{2,1,0:T(8,128)(2,1)S(1)}, bf16[4,512,512]{2,1,0:T(8,128)(2,1)}, u32[]{:S(2)}) copy-start(bf16[4,512,512]{2,1,0:T(8,128)(2,1)} %constant.11.clone.table_ref) | copy-start | bytes 6291460
  70.8 34.4 %copy-start.1 = (f32[7,16,1024]{2,1,0:T(8,128)S(1)}, f32[7,16,1024]{2,1,0:T(8,128)}, u32[]{:S(2)}) copy-start(f32[7,16,1024]{2,1,0:T(8,128)} %re_ref.1) | copy-start | bytes 1376260
  70.8 34.4 %copy-start.2 = (f32[7,16,1024]{2,1,0:T(8,128)S(1)}, f32[7,16,1024]{2,1,0:T(8,128)}, u32[]{:S(2)}) copy-start(f32[7,16,1024]{2,1,0:T(8,128)} %im_ref.1) | copy-start | bytes 1376260
  70.8 34.4 %copy-start.3 = (f32[7,16,1024]{2,1,0:T(8,128)S(1)}, f32[7,16,1024]{2,1,0:T(8,128)}, u32[]{:S(2)}) copy-start(f32[7,16,1024]{2,1,0:T(8,128)} %base_re_ref.1) | copy-start | bytes 1376260
  70.8 34.4 %copy-start.4 = (f32[7,16,1024]{2,1,0:T(8,128)S(1)}, f32[7,16,1024]{2,1,0:T(8,128)}, u32[]{:S(2)}) copy-start(f32[7,16,1024]{2,1,0:T(8,128)} %base_im_ref.1) | copy-start | bytes 1376260

commit v9 on v8

--- a/solution.py
+++ b/solution.py
@@ -193,25 +193,23 @@
 
 
 def points_kernel(
-    in_ref, ahead_ref, triple_ref, back_ref, out_ref, wide_ref, left_ref, phys_ref, keep_ref, flux_ref, half_ref, send_ref
+    in_ref, ahead_ref, triple_ref, back_ref, out_ref, left_ref, phys_ref, keep_ref, flux_ref, half_ref
 ):
     chunk = HALF
     tall = 24 * GROUPS
     masks = lane_masks()
     span = SLABS * OUT
-    for side in range(2):
-        wide_ref[side, span:] = jnp.zeros((16, 128), F32)
 
     def gather(pair, carry):
-        for side in range(2):
-            wide_ref[side, :span] = in_ref[pl.ds(pl.multiple_of((pair * 2 + side) * span, span), span)].astype(F32)
+        held = [in_ref[pl.ds(pl.multiple_of((pair * 2 + side) * span, span), span)] for side in range(2)]
+        nothing = jnp.zeros((24 - OUT, 128), BF)
         for eight in range(SLABS // 8):
             quads = []
             for quad in (2 * eight, 2 * eight + 1):
                 blocks = []
                 for j in range(4):
                     at = (quad * 4 + j) * OUT
-                    blocks.append(jnp.concatenate([wide_ref[side, at : at + 24] for side in range(2)], axis=0).astype(BF))
+                    blocks.append(jnp.concatenate([held[0][at : at + OUT], nothing, held[1][at : at + OUT], nothing], axis=0))
                 quads.append(blocks)
             for part in range(PARTS):
                 mixed = []
@@ -264,22 +262,24 @@
     lax.fori_loop(0, PARTS, line, 0)
     for parity in range(2):
         half_ref[parity] = jnp.dot(flux_ref[parity], back_ref[parity], preferred_element_type=F32)
+    picked = []
     for eight in range(LIVE // 8):
         quads = ([], [])
         for part in range(PARTS):
             rows, lanes = slice(part * 128, (part + 1) * 128), slice(eight * 128, (eight + 1) * 128)
-            for rolled, block in zip(quads, even_odd(half_ref[0, rows, lanes].astype(BF), half_ref[1, rows, lanes].astype(BF))):
+            for rolled, block in zip(
+                quads, even_odd(half_ref[0, rows, lanes].astype(BF), half_ref[1, rows, lanes].astype(BF))
+            ):
                 rolled.append(pltpu.roll(block, 32 * part, 1) if part else block)
-        for quad, rolled in enumerate(quads):
+        for rolled in quads:
             for j in range(4):
-                block = pick(masks, [rolled[(slot - j) % 4] for slot in range(4)]).astype(F32)
-                for group in range(GROUPS):
-                    at = (group * SLABS + eight * 8 + quad * 4 + j) * HOME
-                    send_ref[at : at + HOME] = block[group * 16 : group * 16 + HOME]
+                picked.append(pick(masks, [rolled[(slot - j) % 4] for slot in range(4)]))
+    dead = jnp.zeros(((SLABS - LIVE) * HOME, 128), BF)
     for group in range(GROUPS):
-        at = (group * SLABS + LIVE) * HOME
-        send_ref[at : at + (SLABS - LIVE) * HOME] = jnp.zeros(((SLABS - LIVE) * HOME, 128), F32)
-    out_ref[...] = send_ref[: DEVS * HOME].astype(BF)
+        own = slice(group * 16, group * 16 + HOME)
+        out_ref[group * SLABS * HOME : (group + 1) * SLABS * HOME] = jnp.concatenate(
+            [block[own] for block in picked] + [dead], axis=0
+        )
 
 
 def update_kernel(
@@ -376,13 +376,11 @@
         points_kernel,
         jax.ShapeDtypeStruct((DEVS * HOME, 128), BF),
         [
-            pltpu.VMEM((2, SLABS * OUT + 16, 128), F32),
             pltpu.VMEM((2, PARTS * 24 * GROUPS, KEPT), BF),
             pltpu.VMEM((PARTS * 24 * GROUPS, NG), F32),
             pltpu.VMEM((16 * GROUPS, HALF), F32),
             pltpu.VMEM((2, PARTS * 16 * GROUPS, HALF), BF),
             pltpu.VMEM((2, PARTS * 16 * GROUPS, LIVE * ROWS), F32),
-            pltpu.VMEM((DEVS * HOME + 16, 128), F32),
         ],
         [vmem] * 4,
         10_000_000_000,

time: 108 us -> 107 us (level)
  no operation moved by 1% of the time
where the time goes in v9:
time: 107 us
  blocking collectives  89.5 us (84%)
  Pallas kernels  16.9 us (16%)
    all_to_all x2, blocking collectives, exchange(): lax.all_to_all(blocks, ('mode', 'grid'), split_axis=0, concat_axis=0, til...  89.5 us
    pallas_call x1, Pallas kernels, shards(): call(points_kernel, jax.ShapeDtypeStruct((DEVS * HOME, 128), BF), [pltpu....  10.7 us
    pallas_call x1, Pallas kernels, shards(): call(columns_kernel, jax.ShapeDtypeStruct((DEVS * OUT, 128), BF), [pltpu....  4.09 us
    pallas_call x1, Pallas kernels, shards(): call(update_kernel, (new, new), [pltpu.VMEM((DEVS * HOME + 16, 128), F32)...  2.16 us

profile of v9, /device:TPU:1, one launch (start us, length us, event | category | flops | bytes accessed | tf_op | source)
XLA Modules:
  0.0 107.2 jit_solution(16638411463504419143)
XLA Ops:
  0.6 4.1 %shard_map.104 = bf16[5632,128]{1,0:T(8,128)(2,1)} custom-call(f32[7,16,1024]{2,1,0:T(8,128)} %re_ref.1, f32[7,16,1024]{2,1,0:T(8,128)} %im_ref.1, bf16[4,256,512]{2,1,0:T(8,128)(2,1)} %constant.8.clone.table_hbm), custom_call_target="tpu_custom_call" | custom-call | flops 1000000000 | bytes 4194304 | tf_op jit(solution)/shard_map/pallas_call | solution.py:356
  4.7 0.0 copy-start.5
  4.7 0.0 copy-start.6
  4.8 0.0 copy-start.7
  4.8 55.1 %all_to_all.10 = bf16[256,11,2,128]{3,2,1,0:T(2,128)(2,1)S(1)} all-to-all(bf16[256,11,2,128]{3,2,1,0:T(2,128)(2,1)} %bitcast.9), channel_id=1, replica_groups=mesh['mode'=8,'grid'=32] {'mode','grid'}, dimensions={0} | all-to-all | bytes 2883584 | tf_op jit(solution)/shard_map/all_to_all | solution.py:346
  59.9 0.0 copy-done.5
  59.9 0.0 copy-done.6
  59.9 0.0 copy-done.7
  59.9 0.0 copy-start
  59.9 10.7 %shard_map.105 = bf16[3584,128]{1,0:T(8,128)(2,1)S(1)} custom-call(bf16[5632,128]{1,0:T(8,128)(2,1)S(1)} %bitcast.6, bf16[2,512,512]{2,1,0:T(8,128)(2,1)S(1)} %copy-done.6, bf16[3136,56]{1,0:T(8,128)(2,1)S(1)} %bitcast.8, bf16[2,512,384]{2,1,0:T(8,128)(2,1)S(1)} %copy-done.7), custom_call_target="tpu_custom_call" | custom-call | flops 10000000000 | bytes 4194304 | tf_op jit(solution)/shard_map/pallas_call | solution.py:375
  70.6 0.0 copy-start.1
  70.6 0.0 copy-start.2
  70.6 0.0 copy-start.3
  70.6 0.0 copy-start.4
  70.7 34.4 %all_to_all.11 = bf16[256,7,2,128]{3,2,1,0:T(2,128)(2,1)S(1)} all-to-all(bf16[256,7,2,128]{3,2,1,0:T(2,128)(2,1)S(1)} %bitcast.7), channel_id=1, replica_groups=mesh['mode'=8,'grid'=32] {'mode','grid'}, dimensions={0} | all-to-all | bytes 1835008 | tf_op jit(solution)/shard_map/all_to_all | solution.py:346
  105.0 0.0 copy-done
  105.1 0.0 copy-done.1
  105.1 0.0 copy-done.2
  105.1 0.0 copy-done.3
  105.1 0.0 copy-done.4
  105.1 2.2 %shard_map.106 = (f32[7,16,1024]{2,1,0:T(8,128)}, f32[7,16,1024]{2,1,0:T(8,128)}) custom-call(bf16[3584,128]{1,0:T(8,128)(2,1)S(1)} %bitcast.5, bf16[4,512,512]{2,1,0:T(8,128)(2,1)S(1)} %copy-done, f32[7,16,1024]{2,1,0:T(8,128)S(1)} %copy-done.1, f32[7,16,1024]{2,1,0:T(8,128)S(1)} %copy-done.2, f32[7,16,1024]{2,1,0:T(8,128)S(1)} %copy-done.3, ...), custom_call_target="tpu_custom_call" | custom-call | flops 1000000000 | bytes 4194304 | tf_op jit(solution)/shard_map/pallas_call | solution.py:390
Async XLA Ops:
  4.7 55.2 %copy-start.5 = (bf16[56,56,56]{2,1,0:T(8,128)(2,1)S(1)}, bf16[56,56,56]{2,1,0:T(8,128)(2,1)}, u32[]{:S(2)}) copy-start(bf16[56,56,56]{2,1,0:T(8,128)(2,1)} %param.13) | copy-start | bytes 1053700
  4.7 55.1 %copy-start.6 = (bf16[2,512,512]{2,1,0:T(8,128)(2,1)S(1)}, bf16[2,512,512]{2,1,0:T(8,128)(2,1)}, u32[]{:S(2)}) copy-start(bf16[2,512,512]{2,1,0:T(8,128)(2,1)} %constant.9.clone.ahead_ref) | copy-start | bytes 3145732
  4.8 55.1 %copy-start.7 = (bf16[2,512,384]{2,1,0:T(8,128)(2,1)S(1)}, bf16[2,512,384]{2,1,0:T(8,128)(2,1)}, u32[]{:S(2)}) copy-start(bf16[2,512,384]{2,1,0:T(8,128)(2,1)} %constant.10.clone.back_ref) | copy-start | bytes 2359300
  59.9 45.2 %copy-start = (bf16[4,512,512]{2,1,0:T(8,128)(2,1)S(1)}, bf16[4,512,512]{2,1,0:T(8,128)(2,1)}, u32[]{:S(2)}) copy-start(bf16[4,512,512]{2,1,0:T(8,128)(2,1)} %constant.11.clone.table_ref) | copy-start | bytes 6291460
  70.6 34.4 %copy-start.1 = (f32[7,16,1024]{2,1,0:T(8,128)S(1)}, f32[7,16,1024]{2,1,0:T(8,128)}, u32[]{:S(2)}) copy-start(f32[7,16,1024]{2,1,0:T(8,128)} %re_ref.1) | copy-start | bytes 1376260
  70.6 34.4 %copy-start.2 = (f32[7,16,1024]{2,1,0:T(8,128)S(1)}, f32[7,16,1024]{2,1,0:T(8,128)}, u32[]{:S(2)}) copy-start(f32[7,16,1024]{2,1,0:T(8,128)} %im_ref.1) | copy-start | bytes 1376260
  70.6 34.4 %copy-start.3 = (f32[7,16,1024]{2,1,0:T(8,128)S(1)}, f32[7,16,1024]{2,1,0:T(8,128)}, u32[]{:S(2)}) copy-start(f32[7,16,1024]{2,1,0:T(8,128)} %base_re_ref.1) | copy-start | bytes 1376260
  70.6 34.4 %copy-start.4 = (f32[7,16,1024]{2,1,0:T(8,128)S(1)}, f32[7,16,1024]{2,1,0:T(8,128)}, u32[]{:S(2)}) copy-start(f32[7,16,1024]{2,1,0:T(8,128)} %base_im_ref.1) | copy-start | bytes 1376260

commit v10 on v9

--- a/solution.py
+++ b/solution.py
@@ -309,18 +309,21 @@
                 turn([(prod_ref[part, rows, :QUART], prod_ref[part, rows, QUART:]) for part in range(PARTS)], -1)
             )
         for p in range(4):
-            lanes = slice(p * QUART, (p + 1) * QUART)
-            (x_re, x_im), (y_re, y_im) = spectra[0][p], spectra[1][p]
-            wx, wy = along_x[:, lanes], along_y[:, lanes]
-            adv_re = jnp.where(keep[:, lanes], -(wx * x_im + wy * y_im), 0.0)
-            adv_im = jnp.where(keep[:, lanes], wx * x_re + wy * y_re, 0.0)
-            damp = damping[:, lanes]
-            new_re_ref[mode, :, lanes] = base_re_ref[mode, :, lanes] + STEP_WEIGHT * (
-                -adv_re - damp * re_ref[mode, :, lanes]
-            )
-            new_im_ref[mode, :, lanes] = base_im_ref[mode, :, lanes] + STEP_WEIGHT * (
-                -adv_im - damp * im_ref[mode, :, lanes]
-            )
+            for side in range(2):
+                own = slice(side * HALF // 4, (side + 1) * HALF // 4)
+                at = p * QUART + side * HALF // 4
+                lanes = slice(at, at + HALF // 4)
+                damp = damping[:, lanes]
+                rhs_re = -damp * re_ref[mode, :, lanes]
+                rhs_im = -damp * im_ref[mode, :, lanes]
+                nearest = at if at < HALF else NG - at - HALF // 4 + 1
+                if 3 * nearest < NG:
+                    (x_re, x_im), (y_re, y_im) = [[half[:, own] for half in spectra[g][p]] for g in range(2)]
+                    wx, wy = along_x[:, lanes], along_y[:, lanes]
+                    rhs_re = rhs_re - jnp.where(keep[:, lanes], -(wx * x_im + wy * y_im), 0.0)
+                    rhs_im = rhs_im - jnp.where(keep[:, lanes], wx * x_re + wy * y_re, 0.0)
+                new_re_ref[mode, :, lanes] = base_re_ref[mode, :, lanes] + STEP_WEIGHT * rhs_re
+                new_im_ref[mode, :, lanes] = base_im_ref[mode, :, lanes] + STEP_WEIGHT * rhs_im
         stores.append(pltpu.make_async_copy(new_re_ref.at[mode], new_re.at[mode], sems.at[2 * mode]))
         stores.append(pltpu.make_async_copy(new_im_ref.at[mode], new_im.at[mode], sems.at[2 * mode + 1]))
         stores[-2].start()

time: 107 us -> 107 us (level)
  no operation moved by 1% of the time
where the time goes in v10:
time: 107 us
  blocking collectives  89.5 us (84%)
  Pallas kernels  17 us (16%)
    all_to_all x2, blocking collectives, exchange(): lax.all_to_all(blocks, ('mode', 'grid'), split_axis=0, concat_axis=0, til...  89.5 us
    pallas_call x1, Pallas kernels, shards(): call(points_kernel, jax.ShapeDtypeStruct((DEVS * HOME, 128), BF), [pltpu....  10.7 us
    pallas_call x1, Pallas kernels, shards(): call(columns_kernel, jax.ShapeDtypeStruct((DEVS * OUT, 128), BF), [pltpu....  4.09 us
    pallas_call x1, Pallas kernels, shards(): call(update_kernel, (new, new), [pltpu.VMEM((DEVS * HOME + 16, 128), F32)...  2.17 us

profile of v10, /device:TPU:1, one launch (start us, length us, event | category | flops | bytes accessed | tf_op | source)
XLA Modules:
  0.0 107.3 jit_solution(6714860738137250075)
XLA Ops:
  0.6 4.1 %shard_map.104 = bf16[5632,128]{1,0:T(8,128)(2,1)} custom-call(f32[7,16,1024]{2,1,0:T(8,128)} %re_ref.1, f32[7,16,1024]{2,1,0:T(8,128)} %im_ref.1, bf16[4,256,512]{2,1,0:T(8,128)(2,1)} %constant.8.clone.table_hbm), custom_call_target="tpu_custom_call" | custom-call | flops 1000000000 | bytes 4194304 | tf_op jit(solution)/shard_map/pallas_call | solution.py:359
  4.7 0.0 copy-start.5
  4.7 0.0 copy-start.6
  4.8 0.0 copy-start.7
  4.8 55.1 %all_to_all.10 = bf16[256,11,2,128]{3,2,1,0:T(2,128)(2,1)S(1)} all-to-all(bf16[256,11,2,128]{3,2,1,0:T(2,128)(2,1)} %bitcast.9), channel_id=1, replica_groups=mesh['mode'=8,'grid'=32] {'mode','grid'}, dimensions={0} | all-to-all | bytes 2883584 | tf_op jit(solution)/shard_map/all_to_all | solution.py:349
  59.9 0.0 copy-done.5
  59.9 0.0 copy-done.6
  59.9 0.0 copy-done.7
  59.9 0.0 copy-start
  59.9 10.7 %shard_map.105 = bf16[3584,128]{1,0:T(8,128)(2,1)S(1)} custom-call(bf16[5632,128]{1,0:T(8,128)(2,1)S(1)} %bitcast.6, bf16[2,512,512]{2,1,0:T(8,128)(2,1)S(1)} %copy-done.6, bf16[3136,56]{1,0:T(8,128)(2,1)S(1)} %bitcast.8, bf16[2,512,384]{2,1,0:T(8,128)(2,1)S(1)} %copy-done.7), custom_call_target="tpu_custom_call" | custom-call | flops 10000000000 | bytes 4194304 | tf_op jit(solution)/shard_map/pallas_call | solution.py:378
  70.6 0.0 copy-start.1
  70.6 0.0 copy-start.2
  70.6 0.0 copy-start.3
  70.6 0.0 copy-start.4
  70.7 34.4 %all_to_all.11 = bf16[256,7,2,128]{3,2,1,0:T(2,128)(2,1)S(1)} all-to-all(bf16[256,7,2,128]{3,2,1,0:T(2,128)(2,1)S(1)} %bitcast.7), channel_id=1, replica_groups=mesh['mode'=8,'grid'=32] {'mode','grid'}, dimensions={0} | all-to-all | bytes 1835008 | tf_op jit(solution)/shard_map/all_to_all | solution.py:349
  105.0 0.0 copy-done
  105.1 0.0 copy-done.1
  105.1 0.0 copy-done.2
  105.1 0.0 copy-done.3
  105.1 0.0 copy-done.4
  105.1 2.2 %shard_map.106 = (f32[7,16,1024]{2,1,0:T(8,128)}, f32[7,16,1024]{2,1,0:T(8,128)}) custom-call(bf16[3584,128]{1,0:T(8,128)(2,1)S(1)} %bitcast.5, bf16[4,512,512]{2,1,0:T(8,128)(2,1)S(1)} %copy-done, f32[7,16,1024]{2,1,0:T(8,128)S(1)} %copy-done.1, f32[7,16,1024]{2,1,0:T(8,128)S(1)} %copy-done.2, f32[7,16,1024]{2,1,0:T(8,128)S(1)} %copy-done.3, ...), custom_call_target="tpu_custom_call" | custom-call | flops 1000000000 | bytes 4194304 | tf_op jit(solution)/shard_map/pallas_call | solution.py:393
Async XLA Ops:
  4.7 55.2 %copy-start.5 = (bf16[56,56,56]{2,1,0:T(8,128)(2,1)S(1)}, bf16[56,56,56]{2,1,0:T(8,128)(2,1)}, u32[]{:S(2)}) copy-start(bf16[56,56,56]{2,1,0:T(8,128)(2,1)} %param.13) | copy-start | bytes 1053700
  4.7 55.1 %copy-start.6 = (bf16[2,512,512]{2,1,0:T(8,128)(2,1)S(1)}, bf16[2,512,512]{2,1,0:T(8,128)(2,1)}, u32[]{:S(2)}) copy-start(bf16[2,512,512]{2,1,0:T(8,128)(2,1)} %constant.9.clone.ahead_ref) | copy-start | bytes 3145732
  4.8 55.1 %copy-start.7 = (bf16[2,512,384]{2,1,0:T(8,128)(2,1)S(1)}, bf16[2,512,384]{2,1,0:T(8,128)(2,1)}, u32[]{:S(2)}) copy-start(bf16[2,512,384]{2,1,0:T(8,128)(2,1)} %constant.10.clone.back_ref) | copy-start | bytes 2359300
  59.9 45.2 %copy-start = (bf16[4,512,512]{2,1,0:T(8,128)(2,1)S(1)}, bf16[4,512,512]{2,1,0:T(8,128)(2,1)}, u32[]{:S(2)}) copy-start(bf16[4,512,512]{2,1,0:T(8,128)(2,1)} %constant.11.clone.table_ref) | copy-start | bytes 6291460
  70.6 34.4 %copy-start.1 = (f32[7,16,1024]{2,1,0:T(8,128)S(1)}, f32[7,16,1024]{2,1,0:T(8,128)}, u32[]{:S(2)}) copy-start(f32[7,16,1024]{2,1,0:T(8,128)} %re_ref.1) | copy-start | bytes 1376260
  70.6 34.4 %copy-start.2 = (f32[7,16,1024]{2,1,0:T(8,128)S(1)}, f32[7,16,1024]{2,1,0:T(8,128)}, u32[]{:S(2)}) copy-start(f32[7,16,1024]{2,1,0:T(8,128)} %im_ref.1) | copy-start | bytes 1376260
  70.6 34.4 %copy-start.3 = (f32[7,16,1024]{2,1,0:T(8,128)S(1)}, f32[7,16,1024]{2,1,0:T(8,128)}, u32[]{:S(2)}) copy-start(f32[7,16,1024]{2,1,0:T(8,128)} %base_re_ref.1) | copy-start | bytes 1376260
  70.6 34.4 %copy-start.4 = (f32[7,16,1024]{2,1,0:T(8,128)S(1)}, f32[7,16,1024]{2,1,0:T(8,128)}, u32[]{:S(2)}) copy-start(f32[7,16,1024]{2,1,0:T(8,128)} %base_im_ref.1) | copy-start | bytes 1376260

commit v11 on v9

--- a/solution.py
+++ b/solution.py
@@ -169,7 +169,7 @@
             own = jnp.concatenate(
                 [table_ref[part, :, c * QUART + side * half : c * QUART + (side + 1) * half] for c in range(2)], axis=1
             )
-            prod_ref[side, part] = jnp.dot(left_ref[part], own, preferred_element_type=F32)
+            prod_ref[side, part] = jnp.dot(left_ref[part], own, preferred_element_type=F32).astype(BF)
         for at in range(count):
             rows = slice(at * ROWS, (at + 1) * ROWS)
             block = jnp.concatenate(
@@ -180,7 +180,7 @@
                 ],
                 axis=0,
             )
-            turn_ref[pl.ds(at, half, stride=OUT), :] = block.astype(BF).T.astype(F32)
+            turn_ref[pl.ds(at, half, stride=OUT), :] = block.T.astype(F32)
         send_ref[side] = turn_ref[: half * OUT].astype(BF)
         sends.append(
             pltpu.make_async_copy(
@@ -361,7 +361,7 @@
             pltpu.VMEM((OWN, ROWS, NG), F32),
             pltpu.VMEM((PARTS, 2 * QUART, 2 * QUART), BF),
             pltpu.VMEM((PARTS, count * ROWS, 2 * QUART), BF),
-            pltpu.VMEM((2, PARTS, count * ROWS, QUART), F32),
+            pltpu.VMEM((2, PARTS, count * ROWS, QUART), BF),
             pltpu.VMEM((DEVS // 2 * OUT + 32, 128), F32),
             pltpu.VMEM((2, DEVS // 2 * OUT, 128), BF),
             pltpu.SemaphoreType.DMA((2 * OWN + PARTS + 2,)),

time: 107 us -> 107 us (level)
  no operation moved by 1% of the time
where the time goes in v11:
time: 107 us
  blocking collectives  89.5 us (84%)
  Pallas kernels  16.9 us (16%)
    all_to_all x2, blocking collectives, exchange(): lax.all_to_all(blocks, ('mode', 'grid'), split_axis=0, concat_axis=0, til...  89.5 us
    pallas_call x1, Pallas kernels, shards(): call(points_kernel, jax.ShapeDtypeStruct((DEVS * HOME, 128), BF), [pltpu....  10.7 us
    pallas_call x1, Pallas kernels, shards(): call(columns_kernel, jax.ShapeDtypeStruct((DEVS * OUT, 128), BF), [pltpu....  4.03 us
    pallas_call x1, Pallas kernels, shards(): call(update_kernel, (new, new), [pltpu.VMEM((DEVS * HOME + 16, 128), F32)...  2.16 us

profile of v11, /device:TPU:1, one launch (start us, length us, event | category | flops | bytes accessed | tf_op | source)
XLA Modules:
  0.0 107.2 jit_solution(10906255375562174856)
XLA Ops:
  0.6 4.0 %shard_map.104 = bf16[5632,128]{1,0:T(8,128)(2,1)} custom-call(f32[7,16,1024]{2,1,0:T(8,128)} %re_ref.1, f32[7,16,1024]{2,1,0:T(8,128)} %im_ref.1, bf16[4,256,512]{2,1,0:T(8,128)(2,1)} %constant.8.clone.table_hbm), custom_call_target="tpu_custom_call" | custom-call | flops 1000000000 | bytes 4194304 | tf_op jit(solution)/shard_map/pallas_call | solution.py:356
  4.7 0.0 copy-start.5
  4.7 0.0 copy-start.6
  4.7 0.0 copy-start.7
  4.7 55.1 %all_to_all.10 = bf16[256,11,2,128]{3,2,1,0:T(2,128)(2,1)S(1)} all-to-all(bf16[256,11,2,128]{3,2,1,0:T(2,128)(2,1)} %bitcast.9), channel_id=1, replica_groups=mesh['mode'=8,'grid'=32] {'mode','grid'}, dimensions={0} | all-to-all | bytes 2883584 | tf_op jit(solution)/shard_map/all_to_all | solution.py:346
  59.8 0.0 copy-done.5
  59.8 0.0 copy-done.6
  59.8 0.0 copy-done.7
  59.8 0.0 copy-start
  59.8 10.7 %shard_map.105 = bf16[3584,128]{1,0:T(8,128)(2,1)S(1)} custom-call(bf16[5632,128]{1,0:T(8,128)(2,1)S(1)} %bitcast.6, bf16[2,512,512]{2,1,0:T(8,128)(2,1)S(1)} %copy-done.6, bf16[3136,56]{1,0:T(8,128)(2,1)S(1)} %bitcast.8, bf16[2,512,384]{2,1,0:T(8,128)(2,1)S(1)} %copy-done.7), custom_call_target="tpu_custom_call" | custom-call | flops 10000000000 | bytes 4194304 | tf_op jit(solution)/shard_map/pallas_call | solution.py:375
  70.6 0.0 copy-start.1
  70.6 0.0 copy-start.2
  70.6 0.0 copy-start.3
  70.6 0.0 copy-start.4
  70.6 34.4 %all_to_all.11 = bf16[256,7,2,128]{3,2,1,0:T(2,128)(2,1)S(1)} all-to-all(bf16[256,7,2,128]{3,2,1,0:T(2,128)(2,1)S(1)} %bitcast.7), channel_id=1, replica_groups=mesh['mode'=8,'grid'=32] {'mode','grid'}, dimensions={0} | all-to-all | bytes 1835008 | tf_op jit(solution)/shard_map/all_to_all | solution.py:346
  105.0 0.0 copy-done
  105.0 0.0 copy-done.1
  105.0 0.0 copy-done.2
  105.0 0.0 copy-done.3
  105.0 0.0 copy-done.4
  105.0 2.2 %shard_map.106 = (f32[7,16,1024]{2,1,0:T(8,128)}, f32[7,16,1024]{2,1,0:T(8,128)}) custom-call(bf16[3584,128]{1,0:T(8,128)(2,1)S(1)} %bitcast.5, bf16[4,512,512]{2,1,0:T(8,128)(2,1)S(1)} %copy-done, f32[7,16,1024]{2,1,0:T(8,128)S(1)} %copy-done.1, f32[7,16,1024]{2,1,0:T(8,128)S(1)} %copy-done.2, f32[7,16,1024]{2,1,0:T(8,128)S(1)} %copy-done.3, ...), custom_call_target="tpu_custom_call" | custom-call | flops 1000000000 | bytes 4194304 | tf_op jit(solution)/shard_map/pallas_call | solution.py:390
Async XLA Ops:
  4.7 55.2 %copy-start.5 = (bf16[56,56,56]{2,1,0:T(8,128)(2,1)S(1)}, bf16[56,56,56]{2,1,0:T(8,128)(2,1)}, u32[]{:S(2)}) copy-start(bf16[56,56,56]{2,1,0:T(8,128)(2,1)} %param.13) | copy-start | bytes 1053700
  4.7 55.1 %copy-start.6 = (bf16[2,512,512]{2,1,0:T(8,128)(2,1)S(1)}, bf16[2,512,512]{2,1,0:T(8,128)(2,1)}, u32[]{:S(2)}) copy-start(bf16[2,512,512]{2,1,0:T(8,128)(2,1)} %constant.9.clone.ahead_ref) | copy-start | bytes 3145732
  4.7 55.1 %copy-start.7 = (bf16[2,512,384]{2,1,0:T(8,128)(2,1)S(1)}, bf16[2,512,384]{2,1,0:T(8,128)(2,1)}, u32[]{:S(2)}) copy-start(bf16[2,512,384]{2,1,0:T(8,128)(2,1)} %constant.10.clone.back_ref) | copy-start | bytes 2359300
  59.8 45.2 %copy-start = (bf16[4,512,512]{2,1,0:T(8,128)(2,1)S(1)}, bf16[4,512,512]{2,1,0:T(8,128)(2,1)}, u32[]{:S(2)}) copy-start(bf16[4,512,512]{2,1,0:T(8,128)(2,1)} %constant.11.clone.table_ref) | copy-start | bytes 6291460
  70.6 34.4 %copy-start.1 = (f32[7,16,1024]{2,1,0:T(8,128)S(1)}, f32[7,16,1024]{2,1,0:T(8,128)}, u32[]{:S(2)}) copy-start(f32[7,16,1024]{2,1,0:T(8,128)} %re_ref.1) | copy-start | bytes 1376260
  70.6 34.4 %copy-start.2 = (f32[7,16,1024]{2,1,0:T(8,128)S(1)}, f32[7,16,1024]{2,1,0:T(8,128)}, u32[]{:S(2)}) copy-start(f32[7,16,1024]{2,1,0:T(8,128)} %im_ref.1) | copy-start | bytes 1376260
  70.6 34.4 %copy-start.3 = (f32[7,16,1024]{2,1,0:T(8,128)S(1)}, f32[7,16,1024]{2,1,0:T(8,128)}, u32[]{:S(2)}) copy-start(f32[7,16,1024]{2,1,0:T(8,128)} %base_re_ref.1) | copy-start | bytes 1376260
  70.6 34.4 %copy-start.4 = (f32[7,16,1024]{2,1,0:T(8,128)S(1)}, f32[7,16,1024]{2,1,0:T(8,128)}, u32[]{:S(2)}) copy-start(f32[7,16,1024]{2,1,0:T(8,128)} %base_im_ref.1) | copy-start | bytes 1376260
